TPU v7x, 256 devices: a whole 4x4x8 slice. The times are simulated.
256 devices in a mesh: dp: 32 (over z, x), mp: 8 (over y, core).
Axes of the slice: x: 4, y: 4, z: 8, core: 2. Of those that a mesh axis runs over, the one named last changes fastest.
Arguments:
- tokens: bfloat16 [12288, 8192], P('dp', 'mp'), may hold values from -6 to 6
- frozen_base_weight: bfloat16 [8192, 8192], P('mp', 'dp'), may hold values from -0.0625 to 0.0625
- tenant_down_factors: bfloat16 [64, 8192, 64], P('dp', 'mp'), may hold values from -0.0625 to 0.0625
- tenant_up_factors: bfloat16 [64, 8192, 64], P('dp', 'mp'), may hold values from -0.75 to 0.75
- cotangent: bfloat16 [12288, 8192], P('dp', 'mp'), may hold values from -6 to 6
- block_tenant_index: int32 [96], replicated, may hold values from 0 to 63
- ranks: int32 [64], replicated, may hold values from 8 to 64
Outputs:
- layer_out: bfloat16 [12288, 8192], P('dp', 'mp')
- input_grad: bfloat16 [12288, 8192], P('dp', 'mp')
- down_grad: float32 [64, 8192, 64], P('dp', 'mp')
- up_grad: float32 [64, 8192, 64], P('dp', 'mp')
Inputs may be any that keep to these rules, and one draw needn't show every extreme that they name: `block_tenant_index`: tenant of each block of 128 consecutive rows; some tenants own many blocks, some none. `ranks`: rank columns at or past a tenant's rank are unused.
All inputs are finite; a program needn't handle non-finite values.
Results may differ from a plain program's by a relative error of at most 0.017.
Values may be sent and summed in bfloat16 or wider, within the bound.
A program may use at most 128 MiB of HBM per device.

v0:
```python
import jax
import jax.numpy as jnp
from jax import lax
from jax.sharding import PartitionSpec as P

BLOCK = 128


def local(
    tokens,
    frozen_base_weight,
    tenant_down_factors,
    tenant_up_factors,
    cotangent,
    block_tenant_index,
    ranks,
):
    num_peers = lax.axis_size("dp")
    my_index = lax.axis_index("dp")
    row_count, feat_width = tokens.shape
    block_count = row_count // BLOCK
    held_tenant_count = tenant_down_factors.shape[0]
    rank_padding = tenant_down_factors.shape[2]
    count_of_tenants = held_tenant_count * num_peers
    piece_width = feat_width // num_peers
    block_total = block_count * num_peers
    rank_positions = jnp.arange(rank_padding, dtype=jnp.int32)
    kept_ranks = (rank_positions[None, :] < ranks[:, None]).astype(jnp.float32)
    coef_table = kept_ranks * (16.0 / ranks.astype(jnp.float32))[:, None]
    tenant_range = jnp.arange(count_of_tenants, dtype=jnp.int32)
    my_tenants = lax.dynamic_slice_in_dim(block_tenant_index, my_index * block_count, block_count)
    select_onehot = (my_tenants[:, None] == tenant_range[None, :]).astype(jnp.float32)
    block_coef = jnp.dot(select_onehot, coef_table, precision=lax.Precision.HIGHEST)
    stacked_factors = jnp.concatenate([tenant_down_factors, tenant_up_factors], axis=2)
    split_factors = stacked_factors.reshape(
        held_tenant_count, num_peers, piece_width, 2 * rank_padding
    )
    received = lax.all_to_all(split_factors, "dp", split_axis=1, concat_axis=0, tiled=True)
    piece_table = received.reshape(count_of_tenants, piece_width * 2 * rank_padding)
    selection = block_tenant_index.reshape(num_peers, block_count)
    outgoing = piece_table[selection].reshape(num_peers, block_count, piece_width, 2 * rank_padding)
    arrived = lax.all_to_all(outgoing, "dp", split_axis=0, concat_axis=2, tiled=True)
    factors = arrived.reshape(block_count, feat_width, 2 * rank_padding)
    down_factor = factors[:, :, :rank_padding]
    up_factor = factors[:, :, rank_padding:]
    tok_blocks = tokens.reshape(block_count, BLOCK, feat_width)
    low_partial = jnp.einsum(
        "bid,bdr->bir", tok_blocks, down_factor, preferred_element_type=jnp.float32
    )
    pre_low = lax.psum(low_partial.astype(jnp.bfloat16), "mp").astype(jnp.float32)
    low_rank = (pre_low * block_coef[:, None, :]).astype(jnp.bfloat16)
    weights_all = lax.all_gather(frozen_base_weight, "dp", axis=1, tiled=True)
    base_terms = jnp.dot(tokens, weights_all, preferred_element_type=jnp.float32)
    base_share = lax.psum_scatter(
        base_terms.astype(jnp.bfloat16), "mp", scatter_dimension=1, tiled=True
    ).astype(jnp.float32)
    adapter_out = jnp.einsum(
        "bir,ber->bie", low_rank, up_factor, preferred_element_type=jnp.float32
    )
    layer_out = (base_share + adapter_out.reshape(row_count, feat_width)).astype(jnp.bfloat16)
    cot_blocks = cotangent.reshape(block_count, BLOCK, feat_width)
    dlow_partial = jnp.einsum(
        "bie,ber->bir", cot_blocks, up_factor, preferred_element_type=jnp.float32
    )
    pre_dlow = lax.psum(dlow_partial.astype(jnp.bfloat16), "mp").astype(jnp.float32)
    dlow_rank = (pre_dlow * block_coef[:, None, :]).astype(jnp.bfloat16)
    full_cotangent = lax.all_gather(cotangent, "mp", axis=1, tiled=True)
    base_grad = lax.dot_general(
        full_cotangent, weights_all, (((1,), (1,)), ((), ())), preferred_element_type=jnp.float32
    )
    adapter_grad = jnp.einsum(
        "bir,bdr->bid", dlow_rank, down_factor, preferred_element_type=jnp.float32
    )
    input_grad = (base_grad + adapter_grad.reshape(row_count, feat_width)).astype(jnp.bfloat16)
    block_down = jnp.einsum(
        "bid,bir->bdr", tok_blocks, dlow_rank, preferred_element_type=jnp.float32
    )
    block_up = jnp.einsum("bie,bir->ber", cot_blocks, low_rank, preferred_element_type=jnp.float32)
    block_grads = jnp.concatenate([block_down, block_up], axis=2)
    split_grads = block_grads.reshape(block_count, num_peers, piece_width, 2 * rank_padding)
    grad_arrived = lax.all_to_all(
        split_grads.astype(jnp.bfloat16), "dp", split_axis=1, concat_axis=0, tiled=True
    ).astype(split_grads.dtype)
    grad_rows = grad_arrived.reshape(block_total, piece_width * 2 * rank_padding)
    tenant_onehot = (block_tenant_index[None, :] == tenant_range[:, None]).astype(jnp.float32)
    tenant_sums = jnp.dot(tenant_onehot, grad_rows, precision=lax.Precision.HIGHEST)
    owner_bound = tenant_sums.reshape(num_peers, held_tenant_count, piece_width, 2 * rank_padding)
    owned_grads = lax.all_to_all(
        owner_bound.astype(jnp.bfloat16), "dp", split_axis=0, concat_axis=2, tiled=True
    ).astype(owner_bound.dtype)
    owned_grads = owned_grads.reshape(held_tenant_count, feat_width, 2 * rank_padding)
    down_grad = owned_grads[:, :, :rank_padding]
    up_grad = owned_grads[:, :, rank_padding:]
    return (layer_out, input_grad, down_grad, up_grad)


def solution(mesh):
    return jax.shard_map(
        local,
        mesh=mesh,
        in_specs=(
            P("dp", "mp"),
            P("mp", "dp"),
            P("dp", "mp", None),
            P("dp", "mp", None),
            P("dp", "mp"),
            P(),
            P(),
        ),
        out_specs=(P("dp", "mp"), P("dp", "mp"), P("dp", "mp", None), P("dp", "mp", None)),
        check_vma=False,
    )
```

profile of v0, /device:TPU:1, one launch (start us, length us, event | category | flops | bytes accessed | tf_op | source)
XLA Modules:
  0.0 282.0 jit_solution(3312873384921859337)
XLA Ops:
  8.0 0.0 copy-start
  8.0 0.0 all-gather.3.cloned.1.call-start
  8.1 0.7 all-gather.3.cloned.1.call-update
  8.7 1.2 copy.26
  10.0 1.2 copy.25
  11.2 0.3 pad_maximum_fusion.1
  11.5 0.9 copy.27
  12.4 11.9 %all-to-all-start = ((bf16[2,32,32,128]{3,2,0,1:T(8,128)(2,1)}), bf16[2,32,32,128]{3,2,0,1:T(8,128)(2,1)S(1)}, u32[]{:S(2)}, u32[]{:S(2)}) async-start(bf16[2,32,32,128]{3,2,0,1:T(8,128)(2,1)} %copy.27), calls=%async_computation.1 | async-start | bytes 1048576 | tf_op jit(solution)/shard_map/all_to_all | solution.py:38
  24.2 0.0 all-reduce.3.cloned.1.call-start
  24.3 0.8 reshape.107
  25.1 0.1 reshape.119
  25.2 17.0 %all-to-all-done = bf16[2,32,32,128]{3,2,0,1:T(8,128)(2,1)S(1)} async-done(((bf16[2,32,32,128]{3,2,0,1:T(8,128)(2,1)}), bf16[2,32,32,128]{3,2,0,1:T(8,128)(2,1)S(1)}, u32[]{:S(2)}, u32[]{:S(2)}) %all-to-all-start) | async-done | bytes 524320 | tf_op jit(solution)/shard_map/all_to_all | solution.py:38
  42.2 0.2 copy.54
  42.4 0.0 copy-start.1
  42.4 1.0 gather_fusion
  43.4 0.2 copy.43
  43.6 32.1 %all_to_all.54 = bf16[32,3,32,128]{3,2,1,0:T(8,128)(2,1)S(1)} all-to-all(bf16[32,3,32,128]{3,2,1,0:T(8,128)(2,1)S(1)} %bitcast.90), channel_id=1, replica_groups=mesh['dp'=32,'mp'=8] {'dp'}, dimensions={0} | all-to-all | bytes 1572864 | tf_op jit(solution)/shard_map/all_to_all | solution.py:42
  75.7 0.1 copy.28
  75.8 0.0 copy-done
  75.8 1.1 fusion.4
  76.9 0.0 copy-done.1
  76.9 1.4 fusion.5
  78.3 0.0 all-reduce.3.cloned.1.call-update
  78.3 0.0 all-gather.5.cloned.1.call-start
  78.4 0.7 all-gather.5.cloned.1.call-update
  79.1 0.0 reduce-scatter.2.cloned.1.call-start
  79.2 103.5 %all-gather.3.cloned.1.call-done = bf16[1024,8192]{1,0:T(8,128)(2,1)} async-done(((bf16[1024,256]{1,0:T(8,128)(2,1)}), bf16[1024,8192]{1,0:T(8,128)(2,1)}) %all-gather.3.cloned.1.call-update) | async-done | bytes 16777232 | tf_op jit(solution)/shard_map/all_gather | solution.py:52
  182.6 14.3 %convolution_convert_fusion = bf16[384,8192]{1,0:T(8,128)(2,1)} fusion(bf16[384,1024]{1,0:T(8,128)(2,1)S(1)} %copy-done, bf16[1024,8192]{1,0:T(8,128)(2,1)} %all-gather.3.cloned.1.call-done), kind=kOutput, calls=%fused_computation.1 | convolution fusion | flops 6445596672 | bytes 23855104 | tf_op jit(solution)/shard_map/dot_general | solution.py:53
  196.9 0.0 copy-start.5
  196.9 0.0 copy-start.6
  196.9 0.0 copy-start.2
  196.9 0.0 reduce-scatter.2.cloned.1.call-update
  197.0 0.6 copy-done.5
  197.6 0.1 dynamic_slice.3
  197.7 0.0 copy-done.6
  197.7 0.2 fusion.13
  197.9 0.0 all-reduce.3.cloned.1.call-done
  197.9 0.0 copy-start.4
  197.9 0.3 copy-done.2
  198.2 1.1 fusion.3
  199.3 1.1 fusion.2
  200.4 0.0 copy-start.3
  200.5 0.1 pad_maximum_fusion
  200.5 0.4 copy.31
  200.9 0.9 copy.32
  201.8 4.6 %all-to-all-start.2 = ((bf16[3,32,32,128]{3,2,0,1:T(8,128)(2,1)}), bf16[3,32,32,128]{3,2,0,1:T(8,128)(2,1)S(1)}, u32[]{:S(2)}, u32[]{:S(2)}) async-start(bf16[3,32,32,128]{3,2,0,1:T(8,128)(2,1)} %copy.32), calls=%async_computation.3 | async-start | bytes 1572864 | tf_op jit(solution)/shard_map/all_to_all | solution.py:81
  206.4 17.7 %all-to-all-done.2 = bf16[3,32,32,128]{3,2,0,1:T(8,128)(2,1)S(1)} async-done(((bf16[3,32,32,128]{3,2,0,1:T(8,128)(2,1)}), bf16[3,32,32,128]{3,2,0,1:T(8,128)(2,1)S(1)}, u32[]{:S(2)}, u32[]{:S(2)}) %all-to-all-start.2) | async-done | bytes 786464 | tf_op jit(solution)/shard_map/all_to_all | solution.py:81
  224.2 0.4 convolution_convert_fusion.1
  224.6 1.0 copy.34
  225.6 7.4 %all-to-all-start.3 = ((bf16[32,2,32,128]{3,2,1,0:T(8,128)(2,1)}), bf16[32,2,32,128]{3,2,1,0:T(8,128)(2,1)}, u32[]{:S(2)}, u32[]{:S(2)}) async-start(bf16[32,2,32,128]{3,2,1,0:T(8,128)(2,1)} %copy.34), calls=%async_computation.4 | async-start | bytes 1048576 | tf_op jit(solution)/shard_map/all_to_all | solution.py:88
  232.9 0.0 copy-done.4
  232.9 0.7 fusion.7
  233.7 0.0 copy-done.3
  233.7 1.7 fusion.11
  235.4 10.1 %all-to-all-done.3 = bf16[32,2,32,128]{3,2,1,0:T(8,128)(2,1)} async-done(((bf16[32,2,32,128]{3,2,1,0:T(8,128)(2,1)}), bf16[32,2,32,128]{3,2,1,0:T(8,128)(2,1)}, u32[]{:S(2)}, u32[]{:S(2)}) %all-to-all-start.3) | async-done | bytes 524320 | tf_op jit(solution)/shard_map/all_to_all | solution.py:88
  245.5 1.2 bitcast_convert_fusion
  246.7 1.6 fusion.24
  248.3 2.4 copy.36
  250.7 2.3 copy.37
  253.0 0.0 all-gather.5.cloned.1.call-done
  253.0 19.2 %fusion = bf16[384,1024]{1,0:T(8,128)(2,1)} fusion(f32[3,128,1024]{2,1,0:T(8,128)} %fusion.11, bf16[384,8192]{1,0:T(8,128)(2,1)} %all-gather.5.cloned.1.call-done, bf16[1024,8192]{1,0:T(8,128)(2,1)} %all-gather.3.cloned.1.call-done), kind=kOutput, calls=%fused_computation.3 | convolution fusion | flops 6443237376 | bytes 25427968 | tf_op jit(solution)/shard_map/dot_general | solution.py:68
  272.2 0.0 reduce-scatter.2.cloned.1.call-done
  272.2 2.4 fusion.1
  (4 shorter events, 0.0 us)
Async XLA Ops:
  8.0 67.8 %copy-start = (bf16[384,1024]{1,0:T(8,128)(2,1)S(1)}, bf16[384,1024]{1,0:T(8,128)(2,1)}, u32[]{:S(2)}) copy-start(bf16[384,1024]{1,0:T(8,128)(2,1)} %param.7) | copy-start | bytes 2359300
  8.0 174.6 %all-gather.3.cloned.1.call-start = ((), (), s32[]{:S(2)}) async-start(), calls=%async_computation.5 | async-start | bytes 17301504 | tf_op jit(solution)/shard_map/all_gather | solution.py:52
  12.4 29.8 %all-to-all-start = ((bf16[2,32,32,128]{3,2,0,1:T(8,128)(2,1)}), bf16[2,32,32,128]{3,2,0,1:T(8,128)(2,1)S(1)}, u32[]{:S(2)}, u32[]{:S(2)}) async-start(bf16[2,32,32,128]{3,2,0,1:T(8,128)(2,1)} %copy.27), calls=%async_computation.1 | async-start | bytes 1048576 | tf_op jit(solution)/shard_map/all_to_all | solution.py:38
  24.2 173.6 %all-reduce.3.cloned.1.call-start = ((), (), s32[]{:S(2)}) async-start(), calls=%async_computation.8 | async-start | bytes 196608 | tf_op jit(solution)/shard_map/psum | solution.py:50
  42.4 34.5 %copy-start.1 = (bf16[384,1024]{1,0:T(8,128)(2,1)S(1)}, bf16[384,1024]{1,0:T(8,128)(2,1)}, u32[]{:S(2)}) copy-start(bf16[384,1024]{1,0:T(8,128)(2,1)} %param.11) | copy-start | bytes 2359300
  78.3 174.6 %all-gather.5.cloned.1.call-start = ((), (), s32[]{:S(2)}) async-start(), calls=%async_computation.7 | async-start | bytes 7077888 | tf_op jit(solution)/shard_map/all_gather | solution.py:67
  79.1 193.1 %reduce-scatter.2.cloned.1.call-start = ((), (), s32[]{:S(2)}) async-start(), calls=%async_computation.6 | async-start | bytes 7077888 | tf_op jit(solution)/shard_map/reduce_scatter | solution.py:54
  196.9 0.7 copy-start.5
  196.9 0.7 copy-start.6
  196.9 1.3 copy-start.2
  197.9 35.0 %copy-start.4 = (bf16[3,128,64]{1,2,0:T(8,128)(2,1)S(1)}, bf16[3,128,64]{1,2,0:T(8,128)(2,1)}, u32[]{:S(2)}) copy-start(bf16[3,128,64]{1,2,0:T(8,128)(2,1)} %get-tuple-element.12) | copy-start | bytes 147460
  200.4 33.2 %copy-start.3 = (bf16[3,128,64]{1,2,0:T(8,128)(2,1)S(1)}, bf16[3,128,64]{1,2,0:T(8,128)(2,1)}, u32[]{:S(2)}) copy-start(bf16[3,128,64]{1,2,0:T(8,128)(2,1)} %get-tuple-element.13) | copy-start | bytes 147460
  201.8 22.3 %all-to-all-start.2 = ((bf16[3,32,32,128]{3,2,0,1:T(8,128)(2,1)}), bf16[3,32,32,128]{3,2,0,1:T(8,128)(2,1)S(1)}, u32[]{:S(2)}, u32[]{:S(2)}) async-start(bf16[3,32,32,128]{3,2,0,1:T(8,128)(2,1)} %copy.32), calls=%async_computation.3 | async-start | bytes 1572864 | tf_op jit(solution)/shard_map/all_to_all | solution.py:81
  225.6 19.9 %all-to-all-start.3 = ((bf16[32,2,32,128]{3,2,1,0:T(8,128)(2,1)}), bf16[32,2,32,128]{3,2,1,0:T(8,128)(2,1)}, u32[]{:S(2)}, u32[]{:S(2)}) async-start(bf16[32,2,32,128]{3,2,1,0:T(8,128)(2,1)} %copy.34), calls=%async_computation.4 | async-start | bytes 1048576 | tf_op jit(solution)/shard_map/all_to_all | solution.py:88
Sparse Core Ops, SparseCore 0:
  11.6 170.9 all-gather.2
  184.6 50.5 all-gather.4
Sparse Core Ops, SparseCore 1:
  78.4 62.9 all-reduce.2
  197.1 58.5 reduce-scatter.1
where the time goes:
time: 287 us; the launch traced here: 282 us
  waiting for transfers between devices  150 us (52%)
  matrix products  41.2 us (14%)
  blocking collectives  32.1 us (11%)
  starting transfers between devices  24 us (8%)
  between operations  15.7 us (5%)
  local copies, waits for them, and re-layouts  15.3 us (5%)
  other arithmetic  3.9 us (1%)
    all_gather x1, waiting for transfers between devices, local(): weights_all = lax.all_gather(frozen_base_weight, 'dp', axis=1, tiled=True)  103 us
    all_to_all x1, blocking collectives, local(): lax.all_to_all(outgoing, 'dp', split_axis=0, concat_axis=2, tiled=True)  32.1 us
    dot_general x1, matrix products, local(): lax.dot_general(full_cotangent, weights_all, (((1,), (1,)), ((), ())), pr...  19.2 us
    all_to_all x1, waiting for transfers between devices, local(): lax.all_to_all(split_grads.astype(jnp.bfloat16), 'dp', split_axis=1, conc...  17.7 us
    all_to_all x1, waiting for transfers between devices, local(): lax.all_to_all(split_factors, 'dp', split_axis=1, concat_axis=0, tiled=True)  17 us
    dot_general x1, matrix products, local(): jnp.dot(tokens, weights_all, preferred_element_type=jnp.float32)  14.3 us
    all_to_all x1, starting transfers between devices, local(): lax.all_to_all(split_factors, 'dp', split_axis=1, concat_axis=0, tiled=True)  11.9 us
    all_to_all x1, waiting for transfers between devices, local(): lax.all_to_all(owner_bound.astype(jnp.bfloat16), 'dp', split_axis=0, conc...  10.1 us
  transfers between devices with their start and end apart: 7, of which 4 were waited for; matrix products, arithmetic and copies ran while one was open for 20% of the time, Pallas kernels for 0%

commit v1 on v0

v1 whole, which is shorter than its diff:
```python
import functools

import jax
import jax.numpy as jnp
from jax import lax
from jax.experimental import pallas as pl
from jax.experimental.pallas import tpu as pltpu
from jax.sharding import PartitionSpec as P

MESH = pl.DeviceIdType.MESH
BF = jnp.bfloat16
F32 = jnp.float32
NZ, NX, NY = 8, 4, 4
NT = (((1,), (1,)), ((), ()))


def kernel(
    idx, ranks, tok, w, dn, up, cot,
    o_y, o_g, o_dg, o_ug,
    fs, ft, ss, fac, gs, gr, sel, hs, hr, lp, lr, lo,
    wg, xg, cg, yp, yr, ys, yf, gp, gg, ge, gx,
    s_l, r_l, s_wa, r_wa, s_wb, r_wb, s_wc, r_wc, s_x, r_x, s_c, r_c, s_ca, r_ca,
    s_y, r_y, s_ya, r_ya, s_g, r_g, s_gx, r_gx, s_m, r_m, s_loc,
):
    dp = lax.axis_index("dp")
    mp = lax.axis_index("mp")
    z, x = dp // NX, dp % NX
    y, c = mp // 2, mp % 2
    o = 1 - c
    turn = 1 - 2 * c

    def dev(zz, xx, yy, cc):
        return (zz * NX + xx, yy * 2 + cc)

    def start(src, dst, s_sem, r_sem, device):
        copy = pltpu.make_async_remote_copy(
            src_ref=src, dst_ref=dst, send_sem=s_sem, recv_sem=r_sem,
            device_id=device, device_id_type=MESH,
        )
        copy.start()

    def wait(ref, sem):
        pltpu.make_async_copy(ref, ref, sem).wait()

    def ranks_at(i):
        return pl.ds(pl.multiple_of(16 * i, 16), 16)

    def lanes_at(i):
        return pl.ds(pl.multiple_of(256 * i, 256), 256)

    def half(i):
        return pl.ds(pl.multiple_of(192 * i, 192), 192)

    def dp_peer(k):
        return (z + k // NX) % NZ, (x + k % NX) % NX

    barrier = pltpu.get_barrier_semaphore()

    def greet_dp(k, carry):
        pz, px = dp_peer(k)
        pl.semaphore_signal(barrier, inc=1, device_id=dev(pz, px, y, c), device_id_type=MESH)
        return carry

    def greet_mp(k, carry):
        pl.semaphore_signal(barrier, inc=1, device_id=(dp, (mp + k) % 8), device_id_type=MESH)
        return carry

    def greet_x(k, carry):
        pl.semaphore_signal(barrier, inc=1, device_id=dev(z, (x + k) % NX, y, o), device_id_type=MESH)
        return carry

    lax.fori_loop(1, 32, greet_dp, 0)
    lax.fori_loop(1, 8, greet_mp, 0)
    lax.fori_loop(1, 4, greet_x, 0)

    for j in range(8):
        src = dn if j < 4 else up
        r0 = 16 * (j % 4)
        for i in range(4):
            fs[4 * j + i] = src[:, r0:r0 + 16, 256 * i:256 * i + 256]

    pl.semaphore_wait(barrier, 41)

    def spread(k, carry):
        pz, px = dp_peer(k)
        start(fs.at[pz * NX + px], ft.at[pl.ds(2 * dp, 2)], s_l.at[0], r_l.at[0], dev(pz, px, y, c))
        return carry

    lax.fori_loop(1, 32, spread, 0)
    za, zb = (z + turn + NZ) % NZ, (z - turn + NZ) % NZ
    start(w, wg.at[z, c], s_wa.at[0], r_wa.at[0], dev(za, x, y, c))
    start(w, wg.at[z, c], s_wb.at[0], r_wb.at[0], dev(zb, x, y, c))
    start(w, wg.at[z, c], s_wc.at[0], r_wc.at[0], dev(z, x, y, o))
    xr, xl = (x + 1) % NX, (x + 3) % NX
    for h in range(2):
        rows = tok.at[pl.ds(192 * h, 192)]
        start(rows, xg.at[c, x], s_x.at[h], r_x.at[c], dev(z, xr, y, h))
        start(rows, xg.at[c, x], s_x.at[2 + h], r_x.at[2 + c], dev(z, xl, y, h))
    start(tok.at[half(o)], xg.at[c, x], s_x.at[4], r_x.at[4], dev(z, x, y, o))

    def cot_out(j, carry):
        px, ph = (x + j // 2) % NX, (c + j % 2) % 2
        start(cot.at[half(ph), lanes_at(px)], cg.at[mp, x], s_c.at[j], r_c.at[j], dev(z, px, y, ph))
        return carry

    lax.fori_loop(1, 8, cot_out, 0)
    loc = [
        pltpu.make_async_copy(w, wg.at[z, c], s_loc.at[0]),
        pltpu.make_async_copy(tok.at[half(c)], xg.at[c, x], s_loc.at[1]),
        pltpu.make_async_copy(cot.at[half(c), lanes_at(x)], cg.at[mp, x], s_loc.at[2]),
        pltpu.make_async_copy(fs.at[dp], ft.at[pl.ds(2 * dp, 2)], s_loc.at[3]),
    ]
    for copy in loc:
        copy.start()

    lane = lax.broadcasted_iota(jnp.int32, (8, 1536), 1)

    def place(b, carry):
        return jnp.where(lane // 16 == b, idx[b] * 16 + lane % 16, carry)

    owner_row = lax.fori_loop(0, 96, place, jnp.zeros((8, 1536), jnp.int32))[0:1]

    def fill(i, carry):
        at = lax.broadcasted_iota(jnp.int32, (64, 1536), 0) + i * 64
        sel[pl.ds(pl.multiple_of(i * 64, 64), 64), :] = jnp.where(at == owner_row, 1.0, 0.0).astype(BF)
        return carry

    lax.fori_loop(0, 16, fill, 0)
    for copy in loc:
        copy.wait()

    for j in range(1, 8):
        wait(cg.at[0, 0], r_c.at[j])
    own = cg.at[pl.ds(2 * y, 2)]
    for d in range(1, 4):
        start(own, own, s_ca.at[d - 1], r_ca.at[d - 1], dev(z, x, (y + d) % NY, c))

    wait(xg.at[0, 0], r_x.at[0])
    start(xg.at[0, xl], xg.at[0, xl], s_x.at[5], r_x.at[5], dev(z, xr, y, c))
    wait(xg.at[0, 0], r_x.at[3])
    start(xg.at[1, xr], xg.at[1, xr], s_x.at[6], r_x.at[6], dev(z, xl, y, c))

    def ring(k):
        ca, cb = (z - turn * k + NZ) % NZ, (z + turn * k + NZ) % NZ
        wait(w, r_wa.at[k - 1])
        if k < 4:
            start(wg.at[ca, c], wg.at[ca, c], s_wa.at[k], r_wa.at[k], dev(za, x, y, c))
        start(wg.at[ca, c], wg.at[ca, c], s_wc.at[k], r_wc.at[k], dev(z, x, y, o))
        if k < 4:
            wait(w, r_wb.at[k - 1])
            if k < 3:
                start(wg.at[cb, c], wg.at[cb, c], s_wb.at[k], r_wb.at[k], dev(zb, x, y, c))
            start(wg.at[cb, c], wg.at[cb, c], s_wc.at[4 + k], r_wc.at[4 + k], dev(z, x, y, o))

    def forward(zc):
        acc = jnp.dot(xg[0].reshape(768, 1024), wg[zc, 0], preferred_element_type=F32)
        acc = acc + jnp.dot(xg[1].reshape(768, 1024), wg[zc, 1], preferred_element_type=F32)
        yp[zc] = acc.astype(BF)
        yd = zc // 2

        @pl.when(yd != y)
        def _():
            slot = ((y - yd + NY) % NY - 1) * 2 + zc % 2
            start(yp.at[zc], yr.at[slot], s_y.at[0], r_y.at[0], dev(z, x, yd, c))

    def forward_pair(k):
        wait(w, r_wc.at[4 + k])
        wait(w, r_wc.at[k])

        def one(i, carry):
            forward((z + (2 * i - 1) * turn * k + NZ) % NZ)
            return carry

        lax.fori_loop(0, 2, one, 0)

    ring(1)

    wait(ft.at[pl.ds(0, 62)], r_l.at[0])

    def select(k, carry):
        pz, px = dp_peer(k)
        p = pz * NX + px
        for s in range(3):
            ss[3 * p + s] = ft[idx[3 * p + s]]
        return carry

    lax.fori_loop(0, 32, select, 0)

    def send_selected(k, carry):
        pz, px = dp_peer(k)
        start(ss.at[pl.ds(3 * (pz * NX + px), 3)], fac.at[:, ranks_at(z), lanes_at(x)],
              s_l.at[1], r_l.at[1], dev(pz, px, y, c))
        return carry

    lax.fori_loop(1, 32, send_selected, 0)
    own_sel = pltpu.make_async_copy(
        ss.at[pl.ds(3 * dp, 3)], fac.at[:, ranks_at(z), lanes_at(x)], s_loc.at[0])
    own_sel.start()

    ring(2)
    for j in (1, 2, 4, 5, 6):
        wait(xg.at[0, 0], r_x.at[j])
    wait(w, r_wc.at[0])
    forward(z)
    forward_pair(1)
    own_sel.wait()

    wait(ss.at[pl.ds(0, 93)], r_l.at[1])
    for s in range(3):
        rows = slice(128 * s, 128 * s + 128)
        a = lax.dot_general(tok[rows], fac[s, 0:64], NT, preferred_element_type=F32)
        b = lax.dot_general(cot[rows], fac[s, 64:128], NT, preferred_element_type=F32)
        lp[rows] = jnp.concatenate([a, b], axis=1)

    def piece(m):
        return pl.ds(pl.multiple_of(48 * m, 16), 48)

    def send_low(k, carry):
        m = (mp + k) % 8
        start(lp.at[piece(m)], lr.at[mp], s_m.at[0], r_m.at[0], (dp, m))
        return carry

    lax.fori_loop(1, 8, send_low, 0)
    lr[mp] = lp[piece(mp)]
    wait(lr.at[pl.ds(0, 7)], r_m.at[0])
    total = lr[0]
    for m in range(1, 8):
        total = total + lr[m]
    rank_lane = lax.broadcasted_iota(jnp.int32, (16, 128), 1) % 64
    coefs = []
    for g in range(3):
        block = dp * 3 + (mp * 48 + 16 * g) // 128
        held = jnp.full((16, 128), ranks[idx[block]], jnp.int32)
        coefs.append(jnp.where(rank_lane < held, 16.0 / held.astype(F32), 0.0))
    lo[piece(mp)] = (total * jnp.concatenate(coefs, axis=0)).astype(BF)

    def send_lo(k, carry):
        m = (mp + k) % 8
        start(lo.at[piece(mp)], lo.at[piece(mp)], s_m.at[1], r_m.at[1], (dp, m))
        return carry

    lax.fori_loop(1, 8, send_lo, 0)

    ring(3)
    wait(lo.at[pl.ds(0, 336)], r_m.at[1])

    for s in range(3):
        rows = slice(128 * s, 128 * s + 128)
        turned = lo[rows].astype(F32).T.astype(BF)
        gs[s, 0:64] = jnp.dot(turned[64:128], tok[rows], preferred_element_type=F32).astype(BF)
        gs[s, 64:128] = jnp.dot(turned[0:64], cot[rows], preferred_element_type=F32).astype(BF)

    def send_grads(k, carry):
        pz, px = dp_peer(k)
        start(gs.at[:, ranks_at(pz), lanes_at(px)], gr.at[pl.ds(3 * dp, 3)],
              s_l.at[2], r_l.at[2], dev(pz, px, y, c))
        return carry

    lax.fori_loop(1, 32, send_grads, 0)
    own_grads = pltpu.make_async_copy(
        gs.at[:, ranks_at(z), lanes_at(x)], gr.at[pl.ds(3 * dp, 3)], s_loc.at[1])
    own_grads.start()

    forward_pair(2)
    ring(4)
    forward_pair(3)
    wait(w, r_wc.at[4])
    forward((z + 4) % NZ)

    for d in range(3):
        wait(cg.at[pl.ds(0, 2)], r_ca.at[d])

    def backward(t, carry):
        acc = jnp.zeros((768, 256), F32)
        for n in range(8):
            acc = acc + lax.dot_general(
                cg[n].reshape(768, 256), wg[n, t // 4, lanes_at(t % 4), :], NT,
                preferred_element_type=F32)
        gp[t] = acc.astype(BF).reshape(4, 192, 256)
        for d in (2, 1, 3):
            px = (x + d) % NX
            start(gp.at[t, px], gg.at[3 - d, t], s_g.at[d - 1], r_g.at[3 - d, t], dev(z, px, y, c))
        return carry

    lax.fori_loop(0, 8, backward, 0)

    wait(yr, r_y.at[0])

    def sum_y(i, carry):
        cc, px = i // 4, i % 4
        rows = pl.ds(pl.multiple_of(192 * px, 192), 192)
        acc = yp[2 * y + cc, rows].astype(F32)
        for d in range(3):
            acc = acc + yr[2 * d + cc, rows].astype(F32)
        ys[cc, px] = acc.astype(BF)
        return carry

    lax.fori_loop(0, 8, sum_y, 0)

    def send_base(j, carry):
        px, pc = (x + j // 2) % NX, (c + j % 2) % 2
        start(ys.at[pc, px], yf.at[c, :, lanes_at(x)], s_ya.at[j], r_ya.at[j], dev(z, px, y, pc))
        return carry

    lax.fori_loop(1, 8, send_base, 0)
    own_base = pltpu.make_async_copy(ys.at[c, x], yf.at[c, :, lanes_at(x)], s_loc.at[2])
    own_base.start()

    own_grads.wait()
    wait(gr.at[pl.ds(0, 93)], r_l.at[2])

    def sum_tenants(i, carry):
        rows = pl.ds(pl.multiple_of(256 * i, 256), 256)
        acc = jnp.dot(sel[rows, :], gr[...].reshape(1536, 256), preferred_element_type=F32)
        hs[pl.ds(16 * i, 16)] = acc.astype(BF).reshape(16, 16, 256)
        return carry

    lax.fori_loop(0, 4, sum_tenants, 0)

    def send_sums(k, carry):
        pz, px = dp_peer(k)
        start(hs.at[pl.ds(2 * (pz * NX + px), 2)], hr.at[:, ranks_at(z), lanes_at(x)],
              s_l.at[3], r_l.at[3], dev(pz, px, y, c))
        return carry

    lax.fori_loop(1, 32, send_sums, 0)
    own_sums = pltpu.make_async_copy(
        hs.at[pl.ds(2 * dp, 2)], hr.at[:, ranks_at(z), lanes_at(x)], s_loc.at[3])
    own_sums.start()

    own_base.wait()
    for j in range(1, 8):
        wait(ys.at[0, 0], r_ya.at[j])
    for u in range(6):
        rows = slice(64 * u, 64 * u + 64)
        acc = jnp.dot(lo[rows, 0:64], fac[u // 2, 64:128], preferred_element_type=F32)
        part = slice(64 * (u % 3), 64 * (u % 3) + 64)
        o_y[rows] = (acc + yf[u // 3, part].astype(F32)).astype(BF)

    def sum_x(t):
        acc = gp[t, x].astype(F32)
        for d in range(3):
            acc = acc + gg[d, t].astype(F32)
        return acc

    for i in range(4):
        t = 4 * o + i
        for d in range(3):
            wait(gg.at[0, 0], r_g.at[d, t])
        ge[i] = sum_x(t).astype(BF)
        start(ge.at[i], gx.at[i], s_gx.at[i], r_gx.at[i], dev(z, x, y, o))
    for i in range(4):
        t = 4 * c + i
        for d in range(3):
            wait(gg.at[0, 0], r_g.at[d, t])

    def adapter_grad(h, i, q):
        rows = pl.ds(pl.multiple_of(192 * h + 64 * q, 64), 64)
        low = lo[rows, :][:, 64:128]
        return rows, jnp.dot(low, fac[(192 * h + 64 * q) // 128, 0:64, 256 * i:256 * i + 256],
                             preferred_element_type=F32)

    for i in range(4):
        total = sum_x(4 * c + i)
        for q in range(3):
            rows, acc = adapter_grad(c, i, q)
            o_g[rows, 256 * i:256 * i + 256] = (acc + total[64 * q:64 * q + 64]).astype(BF)
    for i in range(4):
        wait(ge.at[0], r_gx.at[i])
        for q in range(3):
            rows, acc = adapter_grad(o, i, q)
            part = gx[i, 64 * q:64 * q + 64].astype(F32)
            o_g[rows, 256 * i:256 * i + 256] = (acc + part).astype(BF)

    own_sums.wait()
    wait(hs.at[pl.ds(0, 62)], r_l.at[3])
    o_dg[...] = hr[:, 0:64].astype(F32)
    o_ug[...] = hr[:, 64:128].astype(F32)

    wait(ft.at[pl.ds(0, 62)], s_l.at[0])
    wait(ss.at[pl.ds(0, 93)], s_l.at[1])
    wait(gr.at[pl.ds(0, 93)], s_l.at[2])
    wait(hs.at[pl.ds(0, 62)], s_l.at[3])
    wait(lr.at[pl.ds(0, 7)], s_m.at[0])
    wait(lo.at[pl.ds(0, 336)], s_m.at[1])
    for k in range(4):
        wait(w, s_wa.at[k])
    for k in range(3):
        wait(w, s_wb.at[k])
    for k in range(8):
        wait(w, s_wc.at[k])
    for k in range(7):
        wait(xg.at[0, 0], s_x.at[k])
    for k in range(1, 8):
        wait(cg.at[0, 0], s_c.at[k])
        wait(ys.at[0, 0], s_ya.at[k])
    for d in range(3):
        wait(cg.at[pl.ds(0, 2)], s_ca.at[d])
        wait(gg.at[0], s_g.at[d])
    wait(yr, s_y.at[0])
    for i in range(4):
        wait(ge.at[0], s_gx.at[i])


def local(tokens, weight, down, up, cotangent, idx, ranks):
    down_t = jnp.swapaxes(down, 1, 2)
    up_t = jnp.swapaxes(up, 1, 2)
    vmem = pl.BlockSpec(memory_space=pltpu.VMEM)
    smem = pl.BlockSpec(memory_space=pltpu.SMEM)
    buf = lambda *shape: pltpu.VMEM(shape, BF)
    dma = lambda *shape: pltpu.SemaphoreType.DMA(shape)
    scratch = [
        buf(32, 2, 16, 256), buf(64, 16, 256), buf(96, 16, 256), buf(3, 128, 1024),
        buf(3, 128, 1024), buf(96, 16, 256), buf(1024, 1536), buf(64, 16, 256),
        buf(2, 128, 1024), pltpu.VMEM((384, 128), F32), pltpu.VMEM((8, 48, 128), F32),
        buf(384, 128),
        buf(8, 2, 1024, 256), buf(2, 4, 192, 1024), buf(8, 4, 192, 256),
        buf(8, 768, 256), buf(6, 768, 256), buf(2, 4, 192, 256), buf(2, 192, 1024),
        buf(8, 4, 192, 256), buf(3, 8, 192, 256), buf(4, 192, 256), buf(4, 192, 256),
        dma(4), dma(4), dma(4), dma(4), dma(3), dma(3), dma(8), dma(8), dma(7), dma(7),
        dma(8), dma(8), dma(3), dma(3),
        dma(1), dma(1), dma(8), dma(8), dma(3), dma(3, 8), dma(4), dma(4), dma(2), dma(2),
        dma(4),
    ]
    out = jax.ShapeDtypeStruct
    layer_out, input_grad, down_grad, up_grad = pl.pallas_call(
        kernel,
        out_shape=(
            out(tokens.shape, BF), out(cotangent.shape, BF),
            out(down_t.shape, F32), out(up_t.shape, F32),
        ),
        in_specs=[smem, smem] + [vmem] * 5,
        out_specs=(vmem,) * 4,
        scratch_shapes=scratch,
        compiler_params=pltpu.CompilerParams(
            collective_id=0, has_side_effects=True, vmem_limit_bytes=60 * 1024 * 1024),
        cost_estimate=pl.CostEstimate(
            flops=13_500_000_000, bytes_accessed=6_000_000, transcendentals=0),
        name="lora_projection",
    )(idx, ranks, tokens, weight, down_t, up_t, cotangent)
    return layer_out, input_grad, jnp.swapaxes(down_grad, 1, 2), jnp.swapaxes(up_grad, 1, 2)


def solution(mesh):
    return jax.shard_map(
        local,
        mesh=mesh,
        in_specs=(
            P("dp", "mp"),
            P("mp", "dp"),
            P("dp", "mp", None),
            P("dp", "mp", None),
            P("dp", "mp"),
            P(),
            P(),
        ),
        out_specs=(P("dp", "mp"), P("dp", "mp"), P("dp", "mp", None), P("dp", "mp", None)),
        check_vma=False,
    )
```

time: 287 us -> 205 us (0.71); the launches traced: 282 us -> 205 us
  Pallas kernels: 0 us -> 199 us
  waiting for transfers between devices: 150 us -> 0 us
  matrix products: 41.2 us -> 0 us
  blocking collectives: 32.1 us -> 0 us
  starting transfers between devices: 24 us -> 0 us
  between operations: 15.7 us -> 0.65 us
  local copies, waits for them, and re-layouts: 15.3 us -> 5.49 us
  other arithmetic: 3.9 us -> 0 us
    pallas_call x0 -> x1, Pallas kernels: none -> 199 us  [local(): pl.pallas_call(kernel, out_shape=(out(tokens.shape, BF), out(cotangent.sh...]
    all_gather x2 -> x0, waiting for transfers between devices: 103 us -> none  [the longest x1 103 us: local(): weights_all = lax.all_gather(frozen_base_weight, 'dp', axis=1, tiled=True)]
    all_to_all x3 -> x0, waiting for transfers between devices: 44.9 us -> none  [the longest x1 17.7 us: local(): lax.all_to_all(split_grads.astype(jnp.bfloat16), 'dp', split_axis=1, conc...]
    dot_general x10 -> x0, matrix products: 41.2 us -> none  [the longest x1 19.2 us: local(): lax.dot_general(full_cotangent, weights_all, (((1,), (1,)), ((), ())), pr...]
    all_to_all x1 -> x0, blocking collectives: 32.1 us -> none  [local(): lax.all_to_all(outgoing, 'dp', split_axis=0, concat_axis=2, tiled=True)]
    all_to_all x3 -> x0, starting transfers between devices: 23.8 us -> none  [the longest x1 11.9 us: local(): lax.all_to_all(split_factors, 'dp', split_axis=1, concat_axis=0, tiled=True)]
    convert_element_type x2 -> x0, other arithmetic: 3.53 us -> none  [the longest x1 2.37 us: local(): (base_share + adapter_out.reshape(row_count, feat_width)).astype(jnp.bflo...]
    unnamed x20 -> x10, local copies, waits for them, and re-layouts: 8.48 us -> 5.49 us
  transfers between devices with their start and end apart: 7 -> 0, of which waited for: 4 -> 0; matrix products, arithmetic and copies ran while one was open for 20% -> 0% of each run, Pallas kernels for 0% -> 0%
where the time goes in v1:
time: 205 us
  Pallas kernels  199 us (97%)
  local copies, waits for them, and re-layouts  5.49 us (3%)
    pallas_call x1, Pallas kernels, local(): pl.pallas_call(kernel, out_shape=(out(tokens.shape, BF), out(cotangent.sh...  199 us
    unnamed x10, local copies, waits for them, and re-layouts  5.49 us

profile of v1, /device:TPU:1, one launch (start us, length us, event | category | flops | bytes accessed | tf_op | source)
XLA Modules:
  0.0 204.7 jit_solution(4441507788358247202)
XLA Ops:
  0.6 198.6 %lora_projection.1 = (bf16[384,1024]{1,0:T(8,128)(2,1)}, bf16[384,1024]{1,0:T(8,128)(2,1)}, f32[2,64,1024]{2,1,0:T(8,128)}, f32[2,64,1024]{2,1,0:T(8,128)}) custom-call(s32[96]{0:T(128)} %idx.1, s32[64]{0:T(128)} %ranks.1, bf16[384,1024]{1,0:T(8,128)(2,1)} %tok.1, bf16[1024,256]{1,0:T(8,128)(2,1)} %w.1, bf16[2,64,1024]{2,1,0:T(8,128)(2,1)} %bitcast.6, ...), custom_call_target="tpu_custom_call" | custom-call | flops 13500000256 | bytes 6000000 | tf_op jit(solution)/shard_map/lora_projection/pallas_call | solution.py:426
  199.2 0.0 copy-start
  199.2 2.1 %copy.15 = bf16[384,1024]{1,0:T(8,128)(2,1)} copy(bf16[384,1024]{1,0:T(8,128)(2,1)} %get-tuple-element.16) | data formatting | bytes 1572864
  201.4 0.0 copy-done
  201.4 0.0 copy-start.2
  201.4 0.9 copy.16
  202.3 0.4 copy-done.2
  202.7 0.0 copy-start.1
  202.7 0.8 copy.17
  203.5 0.4 copy-done.1
  203.9 0.8 copy.18
Async XLA Ops:
  199.2 2.1 %copy-start = (bf16[384,1024]{1,0:T(8,128)(2,1)S(1)}, bf16[384,1024]{1,0:T(8,128)(2,1)}, u32[]{:S(2)}) copy-start(bf16[384,1024]{1,0:T(8,128)(2,1)} %get-tuple-element.17) | copy-start | bytes 2359300
  201.4 1.3 copy-start.2
  202.7 1.2 copy-start.1

commit v2 on v0

v2 whole, which is shorter than its diff:
```python
import functools

import jax
import jax.numpy as jnp
from jax import lax
from jax.experimental import pallas as pl
from jax.experimental.pallas import tpu as pltpu
from jax.sharding import PartitionSpec as P

MESH = pl.DeviceIdType.MESH
BF = jnp.bfloat16
F32 = jnp.float32
NZ, NX, NY = 8, 4, 4
NT = (((1,), (1,)), ((), ()))


ORDER = (
    ("cot_out",), ("spread",), ("w_own", 0), ("tok_out",), ("own_copies",), ("one_hot",), ("cot_pass",),
    ("ring", 0, 1), ("select",), ("ring", 0, 2), ("w_own", 1), ("tok_pass",), ("ring", 0, 3),
    ("ring", 1, 1), ("ring", 0, 4), ("low",), ("bwd", 0), ("ring", 1, 2), ("low_sum",), ("fwd", 0),
    ("fwd", 1), ("ring", 1, 3), ("grads",), ("fwd", 2), ("ring", 1, 4), ("fwd", 3), ("fwd", 4), ("bwd", 1),
    ("tenant_sums",), ("sum_y",), ("grad_sums", 0), ("grad_result", 0), ("layer_result",),
    ("grad_sums", 1), ("grad_result", 1), ("factor_result",),
)


def kernel(
    idx, ranks, tok, w, dn, up, cot,
    o_y, o_g, o_dg, o_ug,
    fs, ft, ss, fac, gs, gr, sel, hs, hr, lp, lr, lo,
    wg, xg, cg, yp, yr, ys, yf, gp, gg, ge, gx,
    s_l, r_l, s_wa, r_wa, s_wb, r_wb, s_wc, r_wc, s_x, r_x, s_c, r_c, s_ca, r_ca,
    s_y, r_y, s_ya, r_ya, s_g, r_g, s_gx, r_gx, s_m, r_m, s_loc,
):
    dp = lax.axis_index("dp")
    mp = lax.axis_index("mp")
    z, x = dp // NX, dp % NX
    y, c = mp // 2, mp % 2
    o = 1 - c
    turn = 1 - 2 * c

    def dev(zz, xx, yy, cc):
        return (zz * NX + xx, yy * 2 + cc)

    def start(src, dst, s_sem, r_sem, device):
        copy = pltpu.make_async_remote_copy(
            src_ref=src, dst_ref=dst, send_sem=s_sem, recv_sem=r_sem,
            device_id=device, device_id_type=MESH,
        )
        copy.start()

    def wait(ref, sem):
        pltpu.make_async_copy(ref, ref, sem).wait()

    def ranks_at(i):
        return pl.ds(pl.multiple_of(16 * i, 16), 16)

    def lanes_at(i):
        return pl.ds(pl.multiple_of(256 * i, 256), 256)

    def half(i):
        return pl.ds(pl.multiple_of(192 * i, 192), 192)

    def dp_peer(k):
        return (z + k // NX) % NZ, (x + k % NX) % NX

    barrier = pltpu.get_barrier_semaphore()

    def greet_dp(k, carry):
        pz, px = dp_peer(k)
        pl.semaphore_signal(barrier, inc=1, device_id=dev(pz, px, y, c), device_id_type=MESH)
        return carry

    def greet_mp(k, carry):
        pl.semaphore_signal(barrier, inc=1, device_id=(dp, (mp + k) % 8), device_id_type=MESH)
        return carry

    def greet_x(k, carry):
        pl.semaphore_signal(barrier, inc=1, device_id=dev(z, (x + k) % NX, y, o), device_id_type=MESH)
        return carry

    lax.fori_loop(1, 32, greet_dp, 0)
    lax.fori_loop(1, 8, greet_mp, 0)
    lax.fori_loop(1, 4, greet_x, 0)

    for j in range(8):
        src = dn if j < 4 else up
        r0 = 16 * (j % 4)
        for i in range(4):
            fs[4 * j + i] = src[:, r0:r0 + 16, 256 * i:256 * i + 256]

    pl.semaphore_wait(barrier, 41)

    za, zb = (z + turn + NZ) % NZ, (z - turn + NZ) % NZ
    xr, xl = (x + 1) % NX, (x + 3) % NX
    met = set()

    def once(key, ref, sem):
        if key not in met:
            met.add(key)
            wait(ref, sem)

    def spread():
        def one(k, carry):
            pz, px = dp_peer(k)
            start(fs.at[pz * NX + px], ft.at[pl.ds(2 * dp, 2)], s_l.at[0], r_l.at[0], dev(pz, px, y, c))
            return carry

        lax.fori_loop(1, 32, one, 0)
        ft[pl.ds(2 * dp, 2)] = fs[dp]

    def w_own(j):
        rows = pl.ds(512 * j, 512)
        start(w.at[rows], wg.at[z, c, rows], s_wa.at[j, 0], r_wa.at[j, 0], dev(za, x, y, c))
        start(w.at[rows], wg.at[z, c, rows], s_wb.at[j, 0], r_wb.at[j, 0], dev(zb, x, y, c))
        start(w.at[rows], wg.at[z, c, rows], s_wc.at[j, 0], r_wc.at[j, 0], dev(z, x, y, o))

    def ring(j, k):
        rows = pl.ds(512 * j, 512)
        ca, cb = (z - turn * k + NZ) % NZ, (z + turn * k + NZ) % NZ
        a, b = wg.at[ca, c, rows], wg.at[cb, c, rows]
        wait(a, r_wa.at[j, k - 1])
        if k < 4:
            start(a, a, s_wa.at[j, k], r_wa.at[j, k], dev(za, x, y, c))
        start(a, a, s_wc.at[j, k], r_wc.at[j, k], dev(z, x, y, o))
        if k < 4:
            wait(b, r_wb.at[j, k - 1])
            if k < 3:
                start(b, b, s_wb.at[j, k], r_wb.at[j, k], dev(zb, x, y, c))
            start(b, b, s_wc.at[j, 4 + k], r_wc.at[j, 4 + k], dev(z, x, y, o))

    def need_core(j, k):
        once(("core", j, k), w.at[pl.ds(0, 512)], r_wc.at[j, k])

    def tok_out():
        for h in range(2):
            rows = tok.at[pl.ds(192 * h, 192)]
            start(rows, xg.at[c, x], s_x.at[h], r_x.at[c], dev(z, xr, y, h))
            start(rows, xg.at[c, x], s_x.at[2 + h], r_x.at[2 + c], dev(z, xl, y, h))
        start(tok.at[half(o)], xg.at[c, x], s_x.at[4], r_x.at[4], dev(z, x, y, o))

    def tok_pass():
        wait(xg.at[0, 0], r_x.at[0])
        start(xg.at[0, xl], xg.at[0, xl], s_x.at[5], r_x.at[5], dev(z, xr, y, c))
        wait(xg.at[0, 0], r_x.at[3])
        start(xg.at[1, xr], xg.at[1, xr], s_x.at[6], r_x.at[6], dev(z, xl, y, c))

    def need_tok():
        for j in (1, 2, 4, 5, 6):
            once(("tok", j), xg.at[0, 0], r_x.at[j])

    def cot_out():
        def one(j, carry):
            px, ph = (x + j // 2) % NX, (c + j % 2) % 2
            start(cot.at[half(ph), lanes_at(px)], cg.at[mp, x], s_c.at[j], r_c.at[j], dev(z, px, y, ph))
            return carry

        lax.fori_loop(1, 8, one, 0)

    def own_copies():
        copies = [
            pltpu.make_async_copy(w, wg.at[z, c], s_loc.at[0]),
            pltpu.make_async_copy(tok.at[half(c)], xg.at[c, x], s_loc.at[1]),
            pltpu.make_async_copy(cot.at[half(c), lanes_at(x)], cg.at[mp, x], s_loc.at[2]),
        ]
        for copy in copies:
            copy.start()
        for copy in copies:
            copy.wait()

    def cot_pass():
        for j in range(1, 8):
            wait(cg.at[0, 0], r_c.at[j])
        own = cg.at[pl.ds(2 * y, 2)]
        for d in (2, 1, 3):
            start(own, own, s_ca.at[d - 1], r_ca.at[d - 1], dev(z, x, (y + d) % NY, c))

    def need_cot():
        for d in range(3):
            once(("cot", d), cg.at[pl.ds(0, 2)], r_ca.at[d])

    def one_hot():
        lane = lax.broadcasted_iota(jnp.int32, (8, 1536), 1)

        def place(b, carry):
            return jnp.where(lane // 16 == b, idx[b] * 16 + lane % 16, carry)

        owner_row = lax.fori_loop(0, 96, place, jnp.zeros((8, 1536), jnp.int32))[0:1]

        def fill(i, carry):
            at = lax.broadcasted_iota(jnp.int32, (64, 1536), 0) + i * 64
            sel[pl.ds(pl.multiple_of(i * 64, 64), 64), :] = jnp.where(at == owner_row, 1.0, 0.0).astype(BF)
            return carry

        lax.fori_loop(0, 16, fill, 0)

    def forward(zc):
        acc = jnp.dot(xg[0].reshape(768, 1024), wg[zc, 0], preferred_element_type=F32)
        acc = acc + jnp.dot(xg[1].reshape(768, 1024), wg[zc, 1], preferred_element_type=F32)
        yp[zc] = acc.astype(BF)
        yd = zc // 2

        @pl.when(yd != y)
        def _():
            slot = ((y - yd + NY) % NY - 1) * 2 + zc % 2
            start(yp.at[zc], yr.at[slot], s_y.at[0], r_y.at[0], dev(z, x, yd, c))

    def fwd(k):
        need_tok()
        for j in range(2):
            need_core(j, k)
            if 0 < k < 4:
                need_core(j, 4 + k)
        if k in (0, 4):
            forward((z + k) % NZ)
        else:
            def one(i, carry):
                forward((z + (2 * i - 1) * turn * k + NZ) % NZ)
                return carry

            lax.fori_loop(0, 2, one, 0)

    def select():
        wait(ft.at[pl.ds(0, 62)], r_l.at[0])

        def one(k, carry):
            pz, px = dp_peer(k)
            p = pz * NX + px
            for s in range(3):
                ss[3 * p + s] = ft[idx[3 * p + s]]
            return carry

        lax.fori_loop(0, 32, one, 0)

        def send(k, carry):
            pz, px = dp_peer(k)
            start(ss.at[pl.ds(3 * (pz * NX + px), 3)], fac.at[:, ranks_at(z), lanes_at(x)],
                  s_l.at[1], r_l.at[1], dev(pz, px, y, c))
            return carry

        lax.fori_loop(1, 32, send, 0)
        own = pltpu.make_async_copy(
            ss.at[pl.ds(3 * dp, 3)], fac.at[:, ranks_at(z), lanes_at(x)], s_loc.at[0])
        own.start()
        own.wait()

    def piece(m):
        return pl.ds(pl.multiple_of(48 * m, 16), 48)

    def low():
        wait(ss.at[pl.ds(0, 93)], r_l.at[1])
        for s in range(3):
            rows = slice(128 * s, 128 * s + 128)
            a = lax.dot_general(tok[rows], fac[s, 0:64], NT, preferred_element_type=F32)
            b = lax.dot_general(cot[rows], fac[s, 64:128], NT, preferred_element_type=F32)
            lp[rows] = jnp.concatenate([a, b], axis=1)

        def send(k, carry):
            m = (mp + k) % 8
            start(lp.at[piece(m)], lr.at[mp], s_m.at[0], r_m.at[0], (dp, m))
            return carry

        lax.fori_loop(1, 8, send, 0)
        lr[mp] = lp[piece(mp)]

    def low_sum():
        wait(lr.at[pl.ds(0, 7)], r_m.at[0])
        total = lr[0]
        for m in range(1, 8):
            total = total + lr[m]
        rank_lane = lax.broadcasted_iota(jnp.int32, (16, 128), 1) % 64
        coefs = []
        for g in range(3):
            block = dp * 3 + (mp * 48 + 16 * g) // 128
            held = jnp.full((16, 128), ranks[idx[block]], jnp.int32)
            coefs.append(jnp.where(rank_lane < held, 16.0 / held.astype(F32), 0.0))
        lo[piece(mp)] = (total * jnp.concatenate(coefs, axis=0)).astype(BF)

        def send(k, carry):
            start(lo.at[piece(mp)], lo.at[piece(mp)], s_m.at[1], r_m.at[1], (dp, (mp + k) % 8))
            return carry

        lax.fori_loop(1, 8, send, 0)

    def grads():
        wait(lo.at[pl.ds(0, 336)], r_m.at[1])
        for s in range(3):
            rows = slice(128 * s, 128 * s + 128)
            turned = lo[rows].astype(F32).T.astype(BF)
            gs[s, 0:64] = jnp.dot(turned[64:128], tok[rows], preferred_element_type=F32).astype(BF)
            gs[s, 64:128] = jnp.dot(turned[0:64], cot[rows], preferred_element_type=F32).astype(BF)

        def send(k, carry):
            pz, px = dp_peer(k)
            start(gs.at[:, ranks_at(pz), lanes_at(px)], gr.at[pl.ds(3 * dp, 3)],
                  s_l.at[2], r_l.at[2], dev(pz, px, y, c))
            return carry

        lax.fori_loop(1, 32, send, 0)
        own = pltpu.make_async_copy(
            gs.at[:, ranks_at(z), lanes_at(x)], gr.at[pl.ds(3 * dp, 3)], s_loc.at[1])
        own.start()
        own.wait()

    def bwd(j):
        need_cot()
        for k in range(8):
            need_core(j, k)

        def one(i, carry):
            t = 4 * (i // 2) + 2 * j + i % 2
            acc = jnp.zeros((768, 256), F32)
            for n in range(8):
                acc = acc + lax.dot_general(
                    cg[n].reshape(768, 256), wg[n, i // 2, lanes_at(2 * j + i % 2), :], NT,
                    preferred_element_type=F32)
            gp[t] = acc.astype(BF).reshape(4, 192, 256)
            for d in (2, 1, 3):
                px = (x + d) % NX
                start(gp.at[t, px], gg.at[3 - d, t], s_g.at[d - 1], r_g.at[3 - d, t], dev(z, px, y, c))
            return carry

        lax.fori_loop(0, 4, one, 0)

    def sum_y():
        wait(yr, r_y.at[0])

        def one(i, carry):
            cc, px = i // 4, i % 4
            rows = pl.ds(pl.multiple_of(192 * px, 192), 192)
            acc = yp[2 * y + cc, rows].astype(F32)
            for d in range(3):
                acc = acc + yr[2 * d + cc, rows].astype(F32)
            ys[cc, px] = acc.astype(BF)
            return carry

        lax.fori_loop(0, 8, one, 0)

        def send(j, carry):
            px, pc = (x + j // 2) % NX, (c + j % 2) % 2
            start(ys.at[pc, px], yf.at[c, :, lanes_at(x)], s_ya.at[j], r_ya.at[j], dev(z, px, y, pc))
            return carry

        lax.fori_loop(1, 8, send, 0)
        own = pltpu.make_async_copy(ys.at[c, x], yf.at[c, :, lanes_at(x)], s_loc.at[2])
        own.start()
        own.wait()

    def tenant_sums():
        wait(gr.at[pl.ds(0, 93)], r_l.at[2])

        def one(i, carry):
            rows = pl.ds(pl.multiple_of(256 * i, 256), 256)
            acc = jnp.dot(sel[rows, :], gr[...].reshape(1536, 256), preferred_element_type=F32)
            hs[pl.ds(16 * i, 16)] = acc.astype(BF).reshape(16, 16, 256)
            return carry

        lax.fori_loop(0, 4, one, 0)

        def send(k, carry):
            pz, px = dp_peer(k)
            start(hs.at[pl.ds(2 * (pz * NX + px), 2)], hr.at[:, ranks_at(z), lanes_at(x)],
                  s_l.at[3], r_l.at[3], dev(pz, px, y, c))
            return carry

        lax.fori_loop(1, 32, send, 0)
        own = pltpu.make_async_copy(
            hs.at[pl.ds(2 * dp, 2)], hr.at[:, ranks_at(z), lanes_at(x)], s_loc.at[3])
        own.start()
        own.wait()

    def layer_result():
        for j in range(1, 8):
            wait(ys.at[0, 0], r_ya.at[j])
        for u in range(6):
            rows = slice(64 * u, 64 * u + 64)
            acc = jnp.dot(lo[rows, 0:64], fac[u // 2, 64:128], preferred_element_type=F32)
            part = slice(64 * (u % 3), 64 * (u % 3) + 64)
            o_y[rows] = (acc + yf[u // 3, part].astype(F32)).astype(BF)

    def sum_x(t):
        for d in range(3):
            wait(gg.at[0, 0], r_g.at[d, t])
        acc = gp[t, x].astype(F32)
        for d in range(3):
            acc = acc + gg[d, t].astype(F32)
        return acc

    def adapter_grad(h, i, q):
        rows = pl.ds(pl.multiple_of(192 * h + 64 * q, 64), 64)
        part = lo[rows, :][:, 64:128]
        return rows, jnp.dot(part, fac[(192 * h + 64 * q) // 128, 0:64, 256 * i:256 * i + 256],
                             preferred_element_type=F32)

    def grad_sums(j):
        for i in (2 * j, 2 * j + 1):
            ge[i] = sum_x(4 * o + i).astype(BF)
            start(ge.at[i], gx.at[i], s_gx.at[i], r_gx.at[i], dev(z, x, y, o))
        for i in (2 * j, 2 * j + 1):
            total = sum_x(4 * c + i)
            for q in range(3):
                rows, acc = adapter_grad(c, i, q)
                o_g[rows, 256 * i:256 * i + 256] = (acc + total[64 * q:64 * q + 64]).astype(BF)

    def grad_result(j):
        for i in (2 * j, 2 * j + 1):
            wait(ge.at[0], r_gx.at[i])
            for q in range(3):
                rows, acc = adapter_grad(o, i, q)
                part = gx[i, 64 * q:64 * q + 64].astype(F32)
                o_g[rows, 256 * i:256 * i + 256] = (acc + part).astype(BF)

    def factor_result():
        wait(hs.at[pl.ds(0, 62)], r_l.at[3])
        o_dg[...] = hr[:, 0:64].astype(F32)
        o_ug[...] = hr[:, 64:128].astype(F32)

    table = {
        "spread": spread,
        "w_own": w_own,
        "ring": ring,
        "tok_out": tok_out,
        "tok_pass": tok_pass,
        "cot_out": cot_out,
        "own_copies": own_copies,
        "cot_pass": cot_pass,
        "one_hot": one_hot,
        "fwd": fwd,
        "select": select,
        "low": low,
        "low_sum": low_sum,
        "grads": grads,
        "bwd": bwd,
        "sum_y": sum_y,
        "tenant_sums": tenant_sums,
        "layer_result": layer_result,
        "grad_sums": grad_sums,
        "grad_result": grad_result,
        "factor_result": factor_result,
    }
    for name, *at in ORDER:
        table[name](*at)

    wait(ft.at[pl.ds(0, 62)], s_l.at[0])
    wait(ss.at[pl.ds(0, 93)], s_l.at[1])
    wait(gr.at[pl.ds(0, 93)], s_l.at[2])
    wait(hs.at[pl.ds(0, 62)], s_l.at[3])
    wait(lr.at[pl.ds(0, 7)], s_m.at[0])
    wait(lo.at[pl.ds(0, 336)], s_m.at[1])
    for j in range(2):
        rows = w.at[pl.ds(0, 512)]
        for k in range(4):
            wait(rows, s_wa.at[j, k])
        for k in range(3):
            wait(rows, s_wb.at[j, k])
        for k in range(8):
            wait(rows, s_wc.at[j, k])
    for k in range(7):
        wait(xg.at[0, 0], s_x.at[k])
    for k in range(1, 8):
        wait(cg.at[0, 0], s_c.at[k])
        wait(ys.at[0, 0], s_ya.at[k])
    for d in range(3):
        wait(cg.at[pl.ds(0, 2)], s_ca.at[d])
        wait(gg.at[0], s_g.at[d])
    wait(yr, s_y.at[0])
    for i in range(4):
        wait(ge.at[0], s_gx.at[i])


def local(tokens, weight, down, up, cotangent, idx, ranks):
    down_t = jnp.swapaxes(down, 1, 2)
    up_t = jnp.swapaxes(up, 1, 2)
    vmem = pl.BlockSpec(memory_space=pltpu.VMEM)
    smem = pl.BlockSpec(memory_space=pltpu.SMEM)
    buf = lambda *shape: pltpu.VMEM(shape, BF)
    dma = lambda *shape: pltpu.SemaphoreType.DMA(shape)
    scratch = [
        buf(32, 2, 16, 256), buf(64, 16, 256), buf(96, 16, 256), buf(3, 128, 1024),
        buf(3, 128, 1024), buf(96, 16, 256), buf(1024, 1536), buf(64, 16, 256),
        buf(2, 128, 1024), pltpu.VMEM((384, 128), F32), pltpu.VMEM((8, 48, 128), F32),
        buf(384, 128),
        buf(8, 2, 1024, 256), buf(2, 4, 192, 1024), buf(8, 4, 192, 256),
        buf(8, 768, 256), buf(6, 768, 256), buf(2, 4, 192, 256), buf(2, 192, 1024),
        buf(8, 4, 192, 256), buf(3, 8, 192, 256), buf(4, 192, 256), buf(4, 192, 256),
        dma(4), dma(4), dma(2, 4), dma(2, 4), dma(2, 3), dma(2, 3), dma(2, 8), dma(2, 8), dma(7), dma(7),
        dma(8), dma(8), dma(3), dma(3),
        dma(1), dma(1), dma(8), dma(8), dma(3), dma(3, 8), dma(4), dma(4), dma(2), dma(2),
        dma(4),
    ]
    out = jax.ShapeDtypeStruct
    layer_out, input_grad, down_grad, up_grad = pl.pallas_call(
        kernel,
        out_shape=(
            out(tokens.shape, BF), out(cotangent.shape, BF),
            out(down_t.shape, F32), out(up_t.shape, F32),
        ),
        in_specs=[smem, smem] + [vmem] * 5,
        out_specs=(vmem,) * 4,
        scratch_shapes=scratch,
        compiler_params=pltpu.CompilerParams(
            collective_id=0, has_side_effects=True, vmem_limit_bytes=60 * 1024 * 1024),
        cost_estimate=pl.CostEstimate(
            flops=13_500_000_000, bytes_accessed=6_000_000, transcendentals=0),
        name="lora_projection",
    )(idx, ranks, tokens, weight, down_t, up_t, cotangent)
    return layer_out, input_grad, jnp.swapaxes(down_grad, 1, 2), jnp.swapaxes(up_grad, 1, 2)


def solution(mesh):
    return jax.shard_map(
        local,
        mesh=mesh,
        in_specs=(
            P("dp", "mp"),
            P("mp", "dp"),
            P("dp", "mp", None),
            P("dp", "mp", None),
            P("dp", "mp"),
            P(),
            P(),
        ),
        out_specs=(P("dp", "mp"), P("dp", "mp"), P("dp", "mp", None), P("dp", "mp", None)),
        check_vma=False,
    )
```

time: 287 us -> 151 us (0.53)
  the two profiles are of different devices: /device:TPU:1 before, /device:TPU:17 now
where the time goes in v2:
time: 151 us
  Pallas kernels  144 us (95%)
  local copies, waits for them, and re-layouts  5.49 us (4%)
    pallas_call x1, Pallas kernels, local(): pl.pallas_call(kernel, out_shape=(out(tokens.shape, BF), out(cotangent.sh...  144 us
    unnamed x10, local copies, waits for them, and re-layouts  5.49 us

profile of v2, /device:TPU:17, one launch (start us, length us, event | category | flops | bytes accessed | tf_op | source)
XLA Modules:
  0.0 150.6 jit_solution(12255842184877354231)
XLA Ops:
  0.6 144.4 %lora_projection.1 = (bf16[384,1024]{1,0:T(8,128)(2,1)}, bf16[384,1024]{1,0:T(8,128)(2,1)}, f32[2,64,1024]{2,1,0:T(8,128)}, f32[2,64,1024]{2,1,0:T(8,128)}) custom-call(s32[96]{0:T(128)} %idx.1, s32[64]{0:T(128)} %ranks.1, bf16[384,1024]{1,0:T(8,128)(2,1)} %tok.1, bf16[1024,256]{1,0:T(8,128)(2,1)} %w.1, bf16[2,64,1024]{2,1,0:T(8,128)(2,1)} %bitcast.6, ...), custom_call_target="tpu_custom_call" | custom-call | flops 13500000256 | bytes 6000000 | tf_op jit(solution)/shard_map/lora_projection/pallas_call | solution.py:492
  145.1 0.0 copy-start
  145.1 2.1 %copy.15 = bf16[384,1024]{1,0:T(8,128)(2,1)} copy(bf16[384,1024]{1,0:T(8,128)(2,1)} %get-tuple-element.16) | data formatting | bytes 1572864
  147.2 0.0 copy-done
  147.2 0.0 copy-start.2
  147.2 0.9 copy.16
  148.1 0.4 copy-done.2
  148.5 0.0 copy-start.1
  148.5 0.8 copy.17
  149.3 0.4 copy-done.1
  149.8 0.8 copy.18
Async XLA Ops:
  145.1 2.1 %copy-start = (bf16[384,1024]{1,0:T(8,128)(2,1)S(1)}, bf16[384,1024]{1,0:T(8,128)(2,1)}, u32[]{:S(2)}) copy-start(bf16[384,1024]{1,0:T(8,128)(2,1)} %get-tuple-element.17) | copy-start | bytes 2359300
  147.2 1.3 copy-start.2
  148.5 1.2 copy-start.1

commit v3 on v2

--- a/solution.py
+++ b/solution.py
@@ -16,21 +16,23 @@
 
 ORDER = (
     ("cot_out",), ("spread",), ("w_own", 0), ("tok_out",), ("own_copies",), ("one_hot",), ("cot_pass",),
-    ("ring", 0, 1), ("select",), ("ring", 0, 2), ("w_own", 1), ("tok_pass",), ("ring", 0, 3),
-    ("ring", 1, 1), ("ring", 0, 4), ("low",), ("bwd", 0), ("ring", 1, 2), ("low_sum",), ("fwd", 0),
-    ("fwd", 1), ("ring", 1, 3), ("grads",), ("fwd", 2), ("ring", 1, 4), ("fwd", 3), ("fwd", 4), ("bwd", 1),
-    ("tenant_sums",), ("sum_y",), ("grad_sums", 0), ("grad_result", 0), ("layer_result",),
-    ("grad_sums", 1), ("grad_result", 1), ("factor_result",),
+    ("ring", 0, 1), ("select",), ("ring", 0, 2), ("w_own", 1), ("tok_pass",), ("cot_far",), ("ring", 0, 3),
+    ("ring", 1, 1), ("ring", 0, 4), ("low",), ("bwd", 0), ("ring", 1, 2), ("low_sum",), ("bwd_far", 0),
+    ("fwd", 0), ("fwd", 1), ("ring", 1, 3), ("grads",), ("fwd", 2), ("ring", 1, 4), ("fwd", 3), ("fwd", 4),
+    ("bwd", 1), ("fwd_far", 0), ("fwd_far", 1), ("tenant_sums",), ("bwd_far", 1), ("sum_y",),
+    ("grad_sums", 0), ("grad_result", 0), ("layer_result",), ("grad_sums", 1), ("grad_result", 1),
+    ("factor_result",),
 )
 
 
 def kernel(
-    idx, ranks, tok, w, dn, up, cot,
-    o_y, o_g, o_dg, o_ug,
+    idx, ranks, tok_in, w_in, dn_in, up_in, cot_in,
+    y_out, g_out, dg_out, ug_out,
     fs, ft, ss, fac, gs, gr, sel, hs, hr, lp, lr, lo,
-    wg, xg, cg, yp, yr, ys, yf, gp, gg, ge, gx,
+    wg, xg, cg, yp, yt, yr, ys, yf, gp, gt, gg, ge, gx,
+    tok, w, dn, up, cot, o_y, o_g, o_dg, o_ug,
     s_l, r_l, s_wa, r_wa, s_wb, r_wb, s_wc, r_wc, s_x, r_x, s_c, r_c, s_ca, r_ca,
-    s_y, r_y, s_ya, r_ya, s_g, r_g, s_gx, r_gx, s_m, r_m, s_loc,
+    s_y, r_y, r_yt, s_ya, r_ya, s_g, r_g, r_gt, s_gx, r_gx, s_m, r_m, s_loc, s_io,
 ):
     dp = lax.axis_index("dp")
     mp = lax.axis_index("mp")
@@ -64,6 +66,13 @@
     def dp_peer(k):
         return (z + k // NX) % NZ, (x + k % NX) % NX
 
+    loads = [
+        pltpu.make_async_copy(a, b, s_io.at[i])
+        for i, (a, b) in enumerate(((dn_in, dn), (up_in, up), (w_in, w), (cot_in, cot), (tok_in, tok)))
+    ]
+    for load in loads:
+        load.start()
+
     barrier = pltpu.get_barrier_semaphore()
 
     def greet_dp(k, carry):
@@ -83,16 +92,21 @@
     lax.fori_loop(1, 8, greet_mp, 0)
     lax.fori_loop(1, 4, greet_x, 0)
 
+    loads[0].wait()
+    loads[1].wait()
     for j in range(8):
         src = dn if j < 4 else up
         r0 = 16 * (j % 4)
         for i in range(4):
             fs[4 * j + i] = src[:, r0:r0 + 16, 256 * i:256 * i + 256]
 
+    for load in loads[2:]:
+        load.wait()
     pl.semaphore_wait(barrier, 41)
 
     za, zb = (z + turn + NZ) % NZ, (z - turn + NZ) % NZ
     xr, xl = (x + 1) % NX, (x + 3) % NX
+    yu, yl = (y + 1) % NY, (y + 3) % NY
     met = set()
 
     def once(key, ref, sem):
@@ -171,13 +185,20 @@
     def cot_pass():
         for j in range(1, 8):
             wait(cg.at[0, 0], r_c.at[j])
-        own = cg.at[pl.ds(2 * y, 2)]
-        for d in (2, 1, 3):
-            start(own, own, s_ca.at[d - 1], r_ca.at[d - 1], dev(z, x, (y + d) % NY, c))
+        for i in range(2):
+            own = cg.at[2 * y + i]
+            start(own, own, s_ca.at[i], r_ca.at[i], dev(z, x, yu, c))
+            start(own, own, s_ca.at[2 + i], r_ca.at[2 + i], dev(z, x, yl, c))
+
+    def cot_far():
+        once(("cot", 0), cg.at[0], r_ca.at[0])
+        start(cg.at[2 * yl], cg.at[2 * yl], s_ca.at[4], r_ca.at[4], dev(z, x, yu, c))
+        once(("cot", 3), cg.at[0], r_ca.at[3])
+        start(cg.at[2 * yu + 1], cg.at[2 * yu + 1], s_ca.at[5], r_ca.at[5], dev(z, x, yl, c))
 
     def need_cot():
-        for d in range(3):
-            once(("cot", d), cg.at[pl.ds(0, 2)], r_ca.at[d])
+        for d in range(6):
+            once(("cot", d), cg.at[0], r_ca.at[d])
 
     def one_hot():
         lane = lax.broadcasted_iota(jnp.int32, (8, 1536), 1)
@@ -198,12 +219,29 @@
         acc = jnp.dot(xg[0].reshape(768, 1024), wg[zc, 0], preferred_element_type=F32)
         acc = acc + jnp.dot(xg[1].reshape(768, 1024), wg[zc, 1], preferred_element_type=F32)
         yp[zc] = acc.astype(BF)
-        yd = zc // 2
-
-        @pl.when(yd != y)
+        yd, par = zc // 2, zc % 2
+        away = (y - yd + NY) % NY
+
+        @pl.when(away == 2)
         def _():
-            slot = ((y - yd + NY) % NY - 1) * 2 + zc % 2
-            start(yp.at[zc], yr.at[slot], s_y.at[0], r_y.at[0], dev(z, x, yd, c))
+            start(yp.at[zc], yt.at[par], s_y.at[2], r_yt.at[par], dev(z, x, (yd + 1 + 2 * par) % NY, c))
+
+        @pl.when(away == 3 - 2 * par)
+        def _():
+            start(yp.at[zc], yr.at[2 + par], s_y.at[1], r_y.at[1], dev(z, x, yd, c))
+
+    def fwd_far(par):
+        wait(yt.at[0], r_yt.at[par])
+        yd = (y + 3 - 2 * par) % NY
+        zc = 2 * yd + par
+
+        def one(i, carry):
+            rows = pl.ds(pl.multiple_of(192 * i, 192), 192)
+            yp[zc, rows] = (yp[zc, rows].astype(F32) + yt[par, rows].astype(F32)).astype(BF)
+            return carry
+
+        lax.fori_loop(0, 4, one, 0)
+        start(yp.at[zc], yr.at[par], s_y.at[0], r_y.at[0], dev(z, x, yd, c))
 
     def fwd(k):
         need_tok()
@@ -315,21 +353,34 @@
                     cg[n].reshape(768, 256), wg[n, i // 2, lanes_at(2 * j + i % 2), :], NT,
                     preferred_element_type=F32)
             gp[t] = acc.astype(BF).reshape(4, 192, 256)
-            for d in (2, 1, 3):
-                px = (x + d) % NX
-                start(gp.at[t, px], gg.at[3 - d, t], s_g.at[d - 1], r_g.at[3 - d, t], dev(z, px, y, c))
+            odd = i % 2
+            ahead, back = (x + 1 + 2 * odd) % NX, (x + 3 - 2 * odd) % NX
+            start(gp.at[t, (x + 2) % NX], gt.at[t], s_g.at[2], r_gt.at[t], dev(z, ahead, y, c))
+            start(gp.at[t, back], gg.at[1, t], s_g.at[1], r_g.at[1, t], dev(z, back, y, c))
             return carry
 
         lax.fori_loop(0, 4, one, 0)
 
+    def bwd_far(j):
+        def one(i, carry):
+            t = 4 * (i // 2) + 2 * j + i % 2
+            ahead = (x + 1 + 2 * (i % 2)) % NX
+            wait(gt.at[0], r_gt.at[t])
+            gp[t, ahead] = (gp[t, ahead].astype(F32) + gt[t].astype(F32)).astype(BF)
+            start(gp.at[t, ahead], gg.at[0, t], s_g.at[0], r_g.at[0, t], dev(z, ahead, y, c))
+            return carry
+
+        lax.fori_loop(0, 4, one, 0)
+
     def sum_y():
-        wait(yr, r_y.at[0])
+        wait(yr.at[pl.ds(0, 2)], r_y.at[0])
+        wait(yr.at[pl.ds(2, 2)], r_y.at[1])
 
         def one(i, carry):
             cc, px = i // 4, i % 4
             rows = pl.ds(pl.multiple_of(192 * px, 192), 192)
             acc = yp[2 * y + cc, rows].astype(F32)
-            for d in range(3):
+            for d in range(2):
                 acc = acc + yr[2 * d + cc, rows].astype(F32)
             ys[cc, px] = acc.astype(BF)
             return carry
@@ -377,12 +428,13 @@
             acc = jnp.dot(lo[rows, 0:64], fac[u // 2, 64:128], preferred_element_type=F32)
             part = slice(64 * (u % 3), 64 * (u % 3) + 64)
             o_y[rows] = (acc + yf[u // 3, part].astype(F32)).astype(BF)
+        pltpu.make_async_copy(o_y, y_out, s_io.at[5]).start()
 
     def sum_x(t):
-        for d in range(3):
+        for d in range(2):
             wait(gg.at[0, 0], r_g.at[d, t])
         acc = gp[t, x].astype(F32)
-        for d in range(3):
+        for d in range(2):
             acc = acc + gg[d, t].astype(F32)
         return acc
 
@@ -409,11 +461,15 @@
                 rows, acc = adapter_grad(o, i, q)
                 part = gx[i, 64 * q:64 * q + 64].astype(F32)
                 o_g[rows, 256 * i:256 * i + 256] = (acc + part).astype(BF)
+        if j == 1:
+            pltpu.make_async_copy(o_g, g_out, s_io.at[6]).start()
 
     def factor_result():
         wait(hs.at[pl.ds(0, 62)], r_l.at[3])
         o_dg[...] = hr[:, 0:64].astype(F32)
+        pltpu.make_async_copy(o_dg, dg_out, s_io.at[7]).start()
         o_ug[...] = hr[:, 64:128].astype(F32)
+        pltpu.make_async_copy(o_ug, ug_out, s_io.at[8]).start()
 
     table = {
         "spread": spread,
@@ -426,6 +482,9 @@
         "cot_pass": cot_pass,
         "one_hot": one_hot,
         "fwd": fwd,
+        "fwd_far": fwd_far,
+        "bwd_far": bwd_far,
+        "cot_far": cot_far,
         "select": select,
         "low": low,
         "low_sum": low_sum,
@@ -440,6 +499,9 @@
     }
     for name, *at in ORDER:
         table[name](*at)
+
+    for i, (a, b) in enumerate(((o_y, y_out), (o_g, g_out), (o_dg, dg_out), (o_ug, ug_out))):
+        pltpu.make_async_copy(a, b, s_io.at[5 + i]).wait()
 
     wait(ft.at[pl.ds(0, 62)], s_l.at[0])
     wait(ss.at[pl.ds(0, 93)], s_l.at[1])
@@ -460,18 +522,30 @@
     for k in range(1, 8):
         wait(cg.at[0, 0], s_c.at[k])
         wait(ys.at[0, 0], s_ya.at[k])
-    for d in range(3):
-        wait(cg.at[pl.ds(0, 2)], s_ca.at[d])
+    for d in range(6):
+        wait(cg.at[0], s_ca.at[d])
+    for d in range(2):
         wait(gg.at[0], s_g.at[d])
-    wait(yr, s_y.at[0])
+        wait(yr.at[pl.ds(0, 2)], s_y.at[d])
+    wait(gt, s_g.at[2])
+    wait(yt, s_y.at[2])
     for i in range(4):
         wait(ge.at[0], s_gx.at[i])
+
+
+def hand_over(*refs):
+    n = len(refs) // 2
+    copies = [pltpu.make_async_copy(refs[i], refs[n + i], refs[-1].at[i]) for i in range(n)]
+    for copy in copies:
+        copy.start()
+    for copy in copies:
+        copy.wait()
 
 
 def local(tokens, weight, down, up, cotangent, idx, ranks):
     down_t = jnp.swapaxes(down, 1, 2)
     up_t = jnp.swapaxes(up, 1, 2)
-    vmem = pl.BlockSpec(memory_space=pltpu.VMEM)
+    anywhere = pl.BlockSpec(memory_space=pl.ANY)
     smem = pl.BlockSpec(memory_space=pltpu.SMEM)
     buf = lambda *shape: pltpu.VMEM(shape, BF)
     dma = lambda *shape: pltpu.SemaphoreType.DMA(shape)
@@ -481,22 +555,24 @@
         buf(2, 128, 1024), pltpu.VMEM((384, 128), F32), pltpu.VMEM((8, 48, 128), F32),
         buf(384, 128),
         buf(8, 2, 1024, 256), buf(2, 4, 192, 1024), buf(8, 4, 192, 256),
-        buf(8, 768, 256), buf(6, 768, 256), buf(2, 4, 192, 256), buf(2, 192, 1024),
-        buf(8, 4, 192, 256), buf(3, 8, 192, 256), buf(4, 192, 256), buf(4, 192, 256),
+        buf(8, 768, 256), buf(2, 768, 256), buf(4, 768, 256), buf(2, 4, 192, 256), buf(2, 192, 1024),
+        buf(8, 4, 192, 256), buf(8, 192, 256), buf(2, 8, 192, 256), buf(4, 192, 256), buf(4, 192, 256),
+        buf(384, 1024), buf(1024, 256), buf(2, 64, 1024), buf(2, 64, 1024), buf(384, 1024),
+        buf(384, 1024), buf(384, 1024), pltpu.VMEM((2, 64, 1024), F32), pltpu.VMEM((2, 64, 1024), F32),
         dma(4), dma(4), dma(2, 4), dma(2, 4), dma(2, 3), dma(2, 3), dma(2, 8), dma(2, 8), dma(7), dma(7),
-        dma(8), dma(8), dma(3), dma(3),
-        dma(1), dma(1), dma(8), dma(8), dma(3), dma(3, 8), dma(4), dma(4), dma(2), dma(2),
-        dma(4),
+        dma(8), dma(8), dma(6), dma(6),
+        dma(3), dma(2), dma(2), dma(8), dma(8), dma(3), dma(2, 8), dma(8), dma(4), dma(4), dma(2), dma(2),
+        dma(4), dma(9),
     ]
     out = jax.ShapeDtypeStruct
-    layer_out, input_grad, down_grad, up_grad = pl.pallas_call(
+    shapes = (
+        out(tokens.shape, BF), out(cotangent.shape, BF), out(down_t.shape, F32), out(up_t.shape, F32),
+    )
+    results = pl.pallas_call(
         kernel,
-        out_shape=(
-            out(tokens.shape, BF), out(cotangent.shape, BF),
-            out(down_t.shape, F32), out(up_t.shape, F32),
-        ),
-        in_specs=[smem, smem] + [vmem] * 5,
-        out_specs=(vmem,) * 4,
+        out_shape=shapes,
+        in_specs=[smem, smem] + [anywhere] * 5,
+        out_specs=(anywhere,) * 4,
         scratch_shapes=scratch,
         compiler_params=pltpu.CompilerParams(
             collective_id=0, has_side_effects=True, vmem_limit_bytes=60 * 1024 * 1024),
@@ -504,6 +580,14 @@
             flops=13_500_000_000, bytes_accessed=6_000_000, transcendentals=0),
         name="lora_projection",
     )(idx, ranks, tokens, weight, down_t, up_t, cotangent)
+    layer_out, input_grad, down_grad, up_grad = pl.pallas_call(
+        hand_over,
+        out_shape=shapes,
+        in_specs=[anywhere] * 4,
+        out_specs=(anywhere,) * 4,
+        scratch_shapes=[dma(4)],
+        name="hand_over",
+    )(*results)
     return layer_out, input_grad, jnp.swapaxes(down_grad, 1, 2), jnp.swapaxes(up_grad, 1, 2)
 
 

time: 151 us -> 222 us (1.47)
  the two profiles are of different devices: /device:TPU:17 before, /device:TPU:1 now
where the time goes in v3:
time: 222 us; the launch traced here: 221 us
  Pallas kernels  220 us (99%)
    pallas_call x1, Pallas kernels, local(): pl.pallas_call(kernel, out_shape=shapes, in_specs=[smem, smem] + [anywher...  140 us
    pallas_call x1, Pallas kernels, local(): pl.pallas_call(hand_over, out_shape=shapes, in_specs=[anywhere] * 4, out_...  80.5 us

profile of v3, /device:TPU:1, one launch (start us, length us, event | category | flops | bytes accessed | tf_op | source)
XLA Modules:
  0.0 221.0 jit_solution(10319390578617607147)
XLA Ops:
  0.6 139.8 %lora_projection.1 = (bf16[384,1024]{1,0:T(8,128)(2,1)}, bf16[384,1024]{1,0:T(8,128)(2,1)}, f32[2,64,1024]{2,1,0:T(8,128)}, f32[2,64,1024]{2,1,0:T(8,128)}) custom-call(s32[96]{0:T(128)} %idx.1, s32[64]{0:T(128)} %ranks.1, bf16[384,1024]{1,0:T(8,128)(2,1)} %tok_in.1, bf16[1024,256]{1,0:T(8,128)(2,1)} %w_in.1, bf16[2,64,1024]{2,1,0:T(8,128)(2,1)} %bitcast.6, ...), custom_call_target="tpu_custom_call" | custom-call | flops 13500000256 | bytes 6000000 | tf_op jit(solution)/shard_map/lora_projection/pallas_call | solution.py:571
  140.5 80.5 %hand_over.1 = (bf16[384,1024]{1,0:T(8,128)(2,1)}, bf16[384,1024]{1,0:T(8,128)(2,1)}, f32[2,64,1024]{2,1,0:T(8,128)}, f32[2,64,1024]{2,1,0:T(8,128)}) custom-call(bf16[384,1024]{1,0:T(8,128)(2,1)} %get-tuple-element.12.refs_0_, bf16[384,1024]{1,0:T(8,128)(2,1)} %get-tuple-element.13.refs_1_, f32[2,64,1024]{2,1,0:T(8,128)} %get-tuple-element.14.refs_2_, ...), custom_call_target="tpu_custom_call" | custom-call | tf_op jit(solution)/shard_map/hand_over/pallas_call | solution.py:583

commit v4 on v3

--- a/solution.py
+++ b/solution.py
@@ -15,13 +15,13 @@
 
 
 ORDER = (
-    ("cot_out",), ("spread",), ("w_own", 0), ("tok_out",), ("own_copies",), ("one_hot",), ("cot_pass",),
-    ("ring", 0, 1), ("select",), ("ring", 0, 2), ("w_own", 1), ("tok_pass",), ("cot_far",), ("ring", 0, 3),
-    ("ring", 1, 1), ("ring", 0, 4), ("low",), ("bwd", 0), ("ring", 1, 2), ("low_sum",), ("bwd_far", 0),
-    ("fwd", 0), ("fwd", 1), ("ring", 1, 3), ("grads",), ("fwd", 2), ("ring", 1, 4), ("fwd", 3), ("fwd", 4),
-    ("bwd", 1), ("fwd_far", 0), ("fwd_far", 1), ("tenant_sums",), ("bwd_far", 1), ("sum_y",),
-    ("grad_sums", 0), ("grad_result", 0), ("layer_result",), ("grad_sums", 1), ("grad_result", 1),
-    ("factor_result",),
+    ("cot_out",), ("spread",), ("w_own", 0), ("w_own", 1), ("tok_out",), ("own_copies",), ("one_hot",),
+    ("cot_pass",), ("ring", 0, 1), ("select",), ("ring", 1, 1), ("ring", 0, 2), ("tok_pass",),
+    ("cot_far",), ("ring", 1, 2), ("fwd", 0), ("ring", 0, 3), ("fwd", 1), ("ring", 1, 3), ("ring", 0, 4),
+    ("low",), ("bwd", 0), ("low_sum",), ("fwd", 2), ("ring", 1, 4), ("grads",), ("bwd_far", 0), ("fwd", 3),
+    ("fwd", 4), ("bwd", 1), ("fwd_far", 0), ("fwd_far", 1), ("tenant_sums", 0), ("bwd_far", 1),
+    ("tenant_sums", 1), ("sum_y",), ("grad_sums", 0), ("grad_result", 0), ("layer_result",),
+    ("grad_sums", 1), ("grad_result", 1), ("factor_result",),
 )
 
 
@@ -60,11 +60,25 @@
     def lanes_at(i):
         return pl.ds(pl.multiple_of(256 * i, 256), 256)
 
+    def part_at(i, h):
+        return pl.ds(pl.multiple_of(256 * i + 128 * h, 128), 128)
+
     def half(i):
         return pl.ds(pl.multiple_of(192 * i, 192), 192)
 
-    def dp_peer(k):
-        return (z + k // NX) % NZ, (x + k % NX) % NX
+    xs = [x] + [lax.rem(x + d, NX) for d in range(1, NX)]
+
+    def each_dp(act):
+        for d in range(1, NX):
+            act(z, xs[d])
+
+        def one(d, carry):
+            pz = lax.rem(z + d, NZ)
+            for px in xs:
+                act(pz, px)
+            return carry
+
+        lax.fori_loop(1, NZ, one, 0)
 
     loads = [
         pltpu.make_async_copy(a, b, s_io.at[i])
@@ -75,22 +89,14 @@
 
     barrier = pltpu.get_barrier_semaphore()
 
-    def greet_dp(k, carry):
-        pz, px = dp_peer(k)
-        pl.semaphore_signal(barrier, inc=1, device_id=dev(pz, px, y, c), device_id_type=MESH)
-        return carry
-
-    def greet_mp(k, carry):
-        pl.semaphore_signal(barrier, inc=1, device_id=(dp, (mp + k) % 8), device_id_type=MESH)
-        return carry
-
-    def greet_x(k, carry):
-        pl.semaphore_signal(barrier, inc=1, device_id=dev(z, (x + k) % NX, y, o), device_id_type=MESH)
-        return carry
-
-    lax.fori_loop(1, 32, greet_dp, 0)
-    lax.fori_loop(1, 8, greet_mp, 0)
-    lax.fori_loop(1, 4, greet_x, 0)
+    def greet(device):
+        pl.semaphore_signal(barrier, inc=1, device_id=device, device_id_type=MESH)
+
+    each_dp(lambda pz, px: greet(dev(pz, px, y, c)))
+    for k in range(1, 8):
+        greet((dp, lax.rem(mp + k, 8)))
+    for px in xs[1:]:
+        greet(dev(z, px, y, o))
 
     loads[0].wait()
     loads[1].wait()
@@ -115,12 +121,10 @@
             wait(ref, sem)
 
     def spread():
-        def one(k, carry):
-            pz, px = dp_peer(k)
+        def send(pz, px):
             start(fs.at[pz * NX + px], ft.at[pl.ds(2 * dp, 2)], s_l.at[0], r_l.at[0], dev(pz, px, y, c))
-            return carry
-
-        lax.fori_loop(1, 32, one, 0)
+
+        each_dp(send)
         ft[pl.ds(2 * dp, 2)] = fs[dp]
 
     def w_own(j):
@@ -261,22 +265,18 @@
     def select():
         wait(ft.at[pl.ds(0, 62)], r_l.at[0])
 
-        def one(k, carry):
-            pz, px = dp_peer(k)
-            p = pz * NX + px
+        def pick(p):
             for s in range(3):
                 ss[3 * p + s] = ft[idx[3 * p + s]]
-            return carry
-
-        lax.fori_loop(0, 32, one, 0)
-
-        def send(k, carry):
-            pz, px = dp_peer(k)
-            start(ss.at[pl.ds(3 * (pz * NX + px), 3)], fac.at[:, ranks_at(z), lanes_at(x)],
+
+        def send(pz, px):
+            p = pz * NX + px
+            pick(p)
+            start(ss.at[pl.ds(3 * p, 3)], fac.at[:, ranks_at(z), lanes_at(x)],
                   s_l.at[1], r_l.at[1], dev(pz, px, y, c))
-            return carry
-
-        lax.fori_loop(1, 32, send, 0)
+
+        each_dp(send)
+        pick(dp)
         own = pltpu.make_async_copy(
             ss.at[pl.ds(3 * dp, 3)], fac.at[:, ranks_at(z), lanes_at(x)], s_loc.at[0])
         own.start()
@@ -293,12 +293,9 @@
             b = lax.dot_general(cot[rows], fac[s, 64:128], NT, preferred_element_type=F32)
             lp[rows] = jnp.concatenate([a, b], axis=1)
 
-        def send(k, carry):
-            m = (mp + k) % 8
+        for k in range(1, 8):
+            m = lax.rem(mp + k, 8)
             start(lp.at[piece(m)], lr.at[mp], s_m.at[0], r_m.at[0], (dp, m))
-            return carry
-
-        lax.fori_loop(1, 8, send, 0)
         lr[mp] = lp[piece(mp)]
 
     def low_sum():
@@ -314,11 +311,8 @@
             coefs.append(jnp.where(rank_lane < held, 16.0 / held.astype(F32), 0.0))
         lo[piece(mp)] = (total * jnp.concatenate(coefs, axis=0)).astype(BF)
 
-        def send(k, carry):
-            start(lo.at[piece(mp)], lo.at[piece(mp)], s_m.at[1], r_m.at[1], (dp, (mp + k) % 8))
-            return carry
-
-        lax.fori_loop(1, 8, send, 0)
+        for k in range(1, 8):
+            start(lo.at[piece(mp)], lo.at[piece(mp)], s_m.at[1], r_m.at[1], (dp, lax.rem(mp + k, 8)))
 
     def grads():
         wait(lo.at[pl.ds(0, 336)], r_m.at[1])
@@ -328,17 +322,17 @@
             gs[s, 0:64] = jnp.dot(turned[64:128], tok[rows], preferred_element_type=F32).astype(BF)
             gs[s, 64:128] = jnp.dot(turned[0:64], cot[rows], preferred_element_type=F32).astype(BF)
 
-        def send(k, carry):
-            pz, px = dp_peer(k)
-            start(gs.at[:, ranks_at(pz), lanes_at(px)], gr.at[pl.ds(3 * dp, 3)],
-                  s_l.at[2], r_l.at[2], dev(pz, px, y, c))
-            return carry
-
-        lax.fori_loop(1, 32, send, 0)
-        own = pltpu.make_async_copy(
-            gs.at[:, ranks_at(z), lanes_at(x)], gr.at[pl.ds(3 * dp, 3)], s_loc.at[1])
-        own.start()
-        own.wait()
+        for h in range(2):
+            def send(pz, px):
+                start(gs.at[:, ranks_at(pz), part_at(px, h)], gr.at[h, pl.ds(3 * dp, 3)],
+                      s_l.at[2 + h], r_l.at[2 + h], dev(pz, px, y, c))
+
+            each_dp(send)
+        for h in range(2):
+            own = pltpu.make_async_copy(
+                gs.at[:, ranks_at(z), part_at(x, h)], gr.at[h, pl.ds(3 * dp, 3)], s_loc.at[1])
+            own.start()
+            own.wait()
 
     def bwd(j):
         need_cot()
@@ -397,26 +391,24 @@
         own.start()
         own.wait()
 
-    def tenant_sums():
-        wait(gr.at[pl.ds(0, 93)], r_l.at[2])
+    def tenant_sums(h):
+        wait(gr.at[h, pl.ds(0, 93)], r_l.at[2 + h])
 
         def one(i, carry):
             rows = pl.ds(pl.multiple_of(256 * i, 256), 256)
-            acc = jnp.dot(sel[rows, :], gr[...].reshape(1536, 256), preferred_element_type=F32)
-            hs[pl.ds(16 * i, 16)] = acc.astype(BF).reshape(16, 16, 256)
+            acc = jnp.dot(sel[rows, :], gr[h].reshape(1536, 128), preferred_element_type=F32)
+            hs[h, pl.ds(16 * i, 16)] = acc.astype(BF).reshape(16, 16, 128)
             return carry
 
         lax.fori_loop(0, 4, one, 0)
 
-        def send(k, carry):
-            pz, px = dp_peer(k)
-            start(hs.at[pl.ds(2 * (pz * NX + px), 2)], hr.at[:, ranks_at(z), lanes_at(x)],
-                  s_l.at[3], r_l.at[3], dev(pz, px, y, c))
-            return carry
-
-        lax.fori_loop(1, 32, send, 0)
+        def send(pz, px):
+            start(hs.at[h, pl.ds(2 * (pz * NX + px), 2)], hr.at[:, ranks_at(z), part_at(x, h)],
+                  s_l.at[4 + h], r_l.at[4 + h], dev(pz, px, y, c))
+
+        each_dp(send)
         own = pltpu.make_async_copy(
-            hs.at[pl.ds(2 * dp, 2)], hr.at[:, ranks_at(z), lanes_at(x)], s_loc.at[3])
+            hs.at[h, pl.ds(2 * dp, 2)], hr.at[:, ranks_at(z), part_at(x, h)], s_loc.at[3])
         own.start()
         own.wait()
 
@@ -465,7 +457,8 @@
             pltpu.make_async_copy(o_g, g_out, s_io.at[6]).start()
 
     def factor_result():
-        wait(hs.at[pl.ds(0, 62)], r_l.at[3])
+        for h in range(2):
+            wait(hs.at[h, pl.ds(0, 62)], r_l.at[4 + h])
         o_dg[...] = hr[:, 0:64].astype(F32)
         pltpu.make_async_copy(o_dg, dg_out, s_io.at[7]).start()
         o_ug[...] = hr[:, 64:128].astype(F32)
@@ -505,8 +498,9 @@
 
     wait(ft.at[pl.ds(0, 62)], s_l.at[0])
     wait(ss.at[pl.ds(0, 93)], s_l.at[1])
-    wait(gr.at[pl.ds(0, 93)], s_l.at[2])
-    wait(hs.at[pl.ds(0, 62)], s_l.at[3])
+    for h in range(2):
+        wait(gr.at[h, pl.ds(0, 93)], s_l.at[2 + h])
+        wait(hs.at[h, pl.ds(0, 62)], s_l.at[4 + h])
     wait(lr.at[pl.ds(0, 7)], s_m.at[0])
     wait(lo.at[pl.ds(0, 336)], s_m.at[1])
     for j in range(2):
@@ -534,11 +528,15 @@
 
 
 def hand_over(*refs):
-    n = len(refs) // 2
-    copies = [pltpu.make_async_copy(refs[i], refs[n + i], refs[-1].at[i]) for i in range(n)]
-    for copy in copies:
+    held, arrived, left = refs[8:12], refs[12], refs[13]
+    inward = [pltpu.make_async_copy(refs[i], held[i], arrived.at[i]) for i in range(4)]
+    outward = [pltpu.make_async_copy(held[i], refs[4 + i], left.at[i]) for i in range(4)]
+    for copy in inward:
         copy.start()
-    for copy in copies:
+    for i in range(4):
+        inward[i].wait()
+        outward[i].start()
+    for copy in outward:
         copy.wait()
 
 
@@ -551,7 +549,7 @@
     dma = lambda *shape: pltpu.SemaphoreType.DMA(shape)
     scratch = [
         buf(32, 2, 16, 256), buf(64, 16, 256), buf(96, 16, 256), buf(3, 128, 1024),
-        buf(3, 128, 1024), buf(96, 16, 256), buf(1024, 1536), buf(64, 16, 256),
+        buf(3, 128, 1024), buf(2, 96, 16, 128), buf(1024, 1536), buf(2, 64, 16, 128),
         buf(2, 128, 1024), pltpu.VMEM((384, 128), F32), pltpu.VMEM((8, 48, 128), F32),
         buf(384, 128),
         buf(8, 2, 1024, 256), buf(2, 4, 192, 1024), buf(8, 4, 192, 256),
@@ -559,7 +557,7 @@
         buf(8, 4, 192, 256), buf(8, 192, 256), buf(2, 8, 192, 256), buf(4, 192, 256), buf(4, 192, 256),
         buf(384, 1024), buf(1024, 256), buf(2, 64, 1024), buf(2, 64, 1024), buf(384, 1024),
         buf(384, 1024), buf(384, 1024), pltpu.VMEM((2, 64, 1024), F32), pltpu.VMEM((2, 64, 1024), F32),
-        dma(4), dma(4), dma(2, 4), dma(2, 4), dma(2, 3), dma(2, 3), dma(2, 8), dma(2, 8), dma(7), dma(7),
+        dma(6), dma(6), dma(2, 4), dma(2, 4), dma(2, 3), dma(2, 3), dma(2, 8), dma(2, 8), dma(7), dma(7),
         dma(8), dma(8), dma(6), dma(6),
         dma(3), dma(2), dma(2), dma(8), dma(8), dma(3), dma(2, 8), dma(8), dma(4), dma(4), dma(2), dma(2),
         dma(4), dma(9),
@@ -585,7 +583,7 @@
         out_shape=shapes,
         in_specs=[anywhere] * 4,
         out_specs=(anywhere,) * 4,
-        scratch_shapes=[dma(4)],
+        scratch_shapes=[pltpu.VMEM(a.shape, a.dtype) for a in shapes] + [dma(4), dma(4)],
         name="hand_over",
     )(*results)
     return layer_out, input_grad, jnp.swapaxes(down_grad, 1, 2), jnp.swapaxes(up_grad, 1, 2)

time: 222 us -> 140 us (0.63)
  Pallas kernels: 220 us -> 139 us
    pallas_call x1, Pallas kernels: 80.5 us -> 2.69 us  [local(): pl.pallas_call(hand_over, out_shape=shapes, in_specs=[anywhere] * 4, out_...]
    pallas_call x1, Pallas kernels: 140 us -> 136 us  [local(): pl.pallas_call(kernel, out_shape=shapes, in_specs=[smem, smem] + [anywher...]
where the time goes in v4:
time: 140 us; the launch traced here: 139 us
  Pallas kernels  139 us (99%)
    pallas_call x1, Pallas kernels, local(): pl.pallas_call(kernel, out_shape=shapes, in_specs=[smem, smem] + [anywher...  136 us

profile of v4, /device:TPU:1, one launch (start us, length us, event | category | flops | bytes accessed | tf_op | source)
XLA Modules:
  0.0 139.4 jit_solution(236027367664324599)
XLA Ops:
  0.6 136.1 %lora_projection.1 = (bf16[384,1024]{1,0:T(8,128)(2,1)}, bf16[384,1024]{1,0:T(8,128)(2,1)}, f32[2,64,1024]{2,1,0:T(8,128)}, f32[2,64,1024]{2,1,0:T(8,128)}) custom-call(s32[96]{0:T(128)} %idx.1, s32[64]{0:T(128)} %ranks.1, bf16[384,1024]{1,0:T(8,128)(2,1)} %tok_in.1, bf16[1024,256]{1,0:T(8,128)(2,1)} %w_in.1, bf16[2,64,1024]{2,1,0:T(8,128)(2,1)} %bitcast.6, ...), custom_call_target="tpu_custom_call" | custom-call | flops 13500000256 | bytes 6000000 | tf_op jit(solution)/shard_map/lora_projection/pallas_call | solution.py:569
  136.7 2.7 %hand_over.1 = (bf16[384,1024]{1,0:T(8,128)(2,1)}, bf16[384,1024]{1,0:T(8,128)(2,1)}, f32[2,64,1024]{2,1,0:T(8,128)}, f32[2,64,1024]{2,1,0:T(8,128)}) custom-call(bf16[384,1024]{1,0:T(8,128)(2,1)} %get-tuple-element.12.refs_0_, bf16[384,1024]{1,0:T(8,128)(2,1)} %get-tuple-element.13.refs_1_, f32[2,64,1024]{2,1,0:T(8,128)} %get-tuple-element.14.refs_2_, ...), custom_call_target="tpu_custom_call" | custom-call | tf_op jit(solution)/shard_map/hand_over/pallas_call | solution.py:581

commit v5 on v4

--- a/solution.py
+++ b/solution.py
@@ -19,18 +19,18 @@
     ("cot_pass",), ("ring", 0, 1), ("select",), ("ring", 1, 1), ("ring", 0, 2), ("tok_pass",),
     ("cot_far",), ("ring", 1, 2), ("fwd", 0), ("ring", 0, 3), ("fwd", 1), ("ring", 1, 3), ("ring", 0, 4),
     ("low",), ("bwd", 0), ("low_sum",), ("fwd", 2), ("ring", 1, 4), ("grads",), ("bwd_far", 0), ("fwd", 3),
-    ("fwd", 4), ("bwd", 1), ("fwd_far", 0), ("fwd_far", 1), ("tenant_sums", 0), ("bwd_far", 1),
-    ("tenant_sums", 1), ("sum_y",), ("grad_sums", 0), ("grad_result", 0), ("layer_result",),
-    ("grad_sums", 1), ("grad_result", 1), ("factor_result",),
+    ("fwd", 4), ("bwd", 1), ("fwd_far", 0), ("fwd_far", 1), ("tenant_sums", 0), ("bwd_far", 1), ("sum_y",),
+    ("tenant_sums", 1), ("grad_sums", 0), ("grad_result", 0), ("layer_result",), ("grad_sums", 1),
+    ("grad_result", 1), ("factor_result",),
 )
 
 
 def kernel(
     idx, ranks, tok_in, w_in, dn_in, up_in, cot_in,
-    y_out, g_out, dg_out, ug_out,
+    y_out, g_out, f_out,
     fs, ft, ss, fac, gs, gr, sel, hs, hr, lp, lr, lo,
     wg, xg, cg, yp, yt, yr, ys, yf, gp, gt, gg, ge, gx,
-    tok, w, dn, up, cot, o_y, o_g, o_dg, o_ug,
+    tok, w, dn, up, cot, o_y, o_g,
     s_l, r_l, s_wa, r_wa, s_wb, r_wb, s_wc, r_wc, s_x, r_x, s_c, r_c, s_ca, r_ca,
     s_y, r_y, r_yt, s_ya, r_ya, s_g, r_g, r_gt, s_gx, r_gx, s_m, r_m, s_loc, s_io,
 ):
@@ -459,10 +459,7 @@
     def factor_result():
         for h in range(2):
             wait(hs.at[h, pl.ds(0, 62)], r_l.at[4 + h])
-        o_dg[...] = hr[:, 0:64].astype(F32)
-        pltpu.make_async_copy(o_dg, dg_out, s_io.at[7]).start()
-        o_ug[...] = hr[:, 64:128].astype(F32)
-        pltpu.make_async_copy(o_ug, ug_out, s_io.at[8]).start()
+        pltpu.make_async_copy(hr, f_out, s_io.at[7]).start()
 
     table = {
         "spread": spread,
@@ -493,7 +490,7 @@
     for name, *at in ORDER:
         table[name](*at)
 
-    for i, (a, b) in enumerate(((o_y, y_out), (o_g, g_out), (o_dg, dg_out), (o_ug, ug_out))):
+    for i, (a, b) in enumerate(((o_y, y_out), (o_g, g_out), (hr, f_out))):
         pltpu.make_async_copy(a, b, s_io.at[5 + i]).wait()
 
     wait(ft.at[pl.ds(0, 62)], s_l.at[0])
@@ -527,14 +524,24 @@
         wait(ge.at[0], s_gx.at[i])
 
 
-def hand_over(*refs):
-    held, arrived, left = refs[8:12], refs[12], refs[13]
-    inward = [pltpu.make_async_copy(refs[i], held[i], arrived.at[i]) for i in range(4)]
-    outward = [pltpu.make_async_copy(held[i], refs[4 + i], left.at[i]) for i in range(4)]
+def hand_over(y_in, g_in, f_in, y_out, g_out, dg_out, ug_out, y, g, f, dg, ug, arrived, left):
+    inward = [
+        pltpu.make_async_copy(a, b, arrived.at[i])
+        for i, (a, b) in enumerate(((f_in, f), (y_in, y), (g_in, g)))
+    ]
+    outward = [
+        pltpu.make_async_copy(a, b, left.at[i])
+        for i, (a, b) in enumerate(((y, y_out), (g, g_out), (dg, dg_out), (ug, ug_out)))
+    ]
     for copy in inward:
         copy.start()
-    for i in range(4):
-        inward[i].wait()
+    inward[0].wait()
+    dg[...] = f[:, 0:64].astype(F32)
+    outward[2].start()
+    ug[...] = f[:, 64:128].astype(F32)
+    outward[3].start()
+    for i in range(2):
+        inward[1 + i].wait()
         outward[i].start()
     for copy in outward:
         copy.wait()
@@ -556,7 +563,7 @@
         buf(8, 768, 256), buf(2, 768, 256), buf(4, 768, 256), buf(2, 4, 192, 256), buf(2, 192, 1024),
         buf(8, 4, 192, 256), buf(8, 192, 256), buf(2, 8, 192, 256), buf(4, 192, 256), buf(4, 192, 256),
         buf(384, 1024), buf(1024, 256), buf(2, 64, 1024), buf(2, 64, 1024), buf(384, 1024),
-        buf(384, 1024), buf(384, 1024), pltpu.VMEM((2, 64, 1024), F32), pltpu.VMEM((2, 64, 1024), F32),
+        buf(384, 1024), buf(384, 1024),
         dma(6), dma(6), dma(2, 4), dma(2, 4), dma(2, 3), dma(2, 3), dma(2, 8), dma(2, 8), dma(7), dma(7),
         dma(8), dma(8), dma(6), dma(6),
         dma(3), dma(2), dma(2), dma(8), dma(8), dma(3), dma(2, 8), dma(8), dma(4), dma(4), dma(2), dma(2),
@@ -566,11 +573,12 @@
     shapes = (
         out(tokens.shape, BF), out(cotangent.shape, BF), out(down_t.shape, F32), out(up_t.shape, F32),
     )
+    factors = out((2, 128, 1024), BF)
     results = pl.pallas_call(
         kernel,
-        out_shape=shapes,
+        out_shape=shapes[:2] + (factors,),
         in_specs=[smem, smem] + [anywhere] * 5,
-        out_specs=(anywhere,) * 4,
+        out_specs=(anywhere,) * 3,
         scratch_shapes=scratch,
         compiler_params=pltpu.CompilerParams(
             collective_id=0, has_side_effects=True, vmem_limit_bytes=60 * 1024 * 1024),
@@ -581,9 +589,11 @@
     layer_out, input_grad, down_grad, up_grad = pl.pallas_call(
         hand_over,
         out_shape=shapes,
-        in_specs=[anywhere] * 4,
+        in_specs=[anywhere] * 3,
         out_specs=(anywhere,) * 4,
-        scratch_shapes=[pltpu.VMEM(a.shape, a.dtype) for a in shapes] + [dma(4), dma(4)],
+        scratch_shapes=[
+            pltpu.VMEM(a.shape, a.dtype) for a in shapes[:2] + (factors,) + shapes[2:]
+        ] + [dma(3), dma(4)],
         name="hand_over",
     )(*results)
     return layer_out, input_grad, jnp.swapaxes(down_grad, 1, 2), jnp.swapaxes(up_grad, 1, 2)

time: 140 us -> 139 us (level)
  no operation moved by 1% of the time
where the time goes in v5:
time: 139 us
  Pallas kernels  138 us (99%)
    pallas_call x1, Pallas kernels, local(): pl.pallas_call(kernel, out_shape=shapes[:2] + (factors,), in_specs=[smem,...  136 us

profile of v5, /device:TPU:1, one launch (start us, length us, event | category | flops | bytes accessed | tf_op | source)
XLA Modules:
  0.0 139.1 jit_solution(3988970938198890919)
XLA Ops:
  0.6 135.8 %lora_projection.1 = (bf16[384,1024]{1,0:T(8,128)(2,1)}, bf16[384,1024]{1,0:T(8,128)(2,1)}, bf16[2,128,1024]{2,1,0:T(8,128)(2,1)}) custom-call(s32[96]{0:T(128)} %idx.1, s32[64]{0:T(128)} %ranks.1, bf16[384,1024]{1,0:T(8,128)(2,1)} %tok_in.1, bf16[1024,256]{1,0:T(8,128)(2,1)} %w_in.1, bf16[2,64,1024]{2,1,0:T(8,128)(2,1)} %bitcast.6, ...), custom_call_target="tpu_custom_call" | custom-call | flops 13500000256 | bytes 6000000 | tf_op jit(solution)/shard_map/lora_projection/pallas_call | solution.py:577
  136.5 2.6 %hand_over.1 = (bf16[384,1024]{1,0:T(8,128)(2,1)}, bf16[384,1024]{1,0:T(8,128)(2,1)}, f32[2,64,1024]{2,1,0:T(8,128)}, f32[2,64,1024]{2,1,0:T(8,128)}) custom-call(bf16[384,1024]{1,0:T(8,128)(2,1)} %get-tuple-element.11.y_in, bf16[384,1024]{1,0:T(8,128)(2,1)} %get-tuple-element.12.g_in, bf16[2,128,1024]{2,1,0:T(8,128)(2,1)} %get-tuple-element.13.f_in), custom_call_target="tpu_custom_call" | custom-call | tf_op jit(solution)/shard_map/hand_over/pallas_call | solution.py:589
